TPU v7x, 32 devices: a whole 2x2x4 slice. The times are simulated.
32 devices in a mesh: gx: 4 (over z), gy: 8 (over y, x, core).
Axes of the slice: x: 2, y: 2, z: 4, core: 2. Of those that a mesh axis runs over, the one named last changes fastest.
Arguments:
- tokens: bfloat16 [2, 12288, 1024], P(None, ('gx', 'gy')), may hold values from -6 to 6
- cotangent: bfloat16 [2, 12288, 1024], P(None, ('gx', 'gy')), may hold values from -6 to 6
- image_ids: int32 [2, 8, 1536], P(None, 'gy'), may hold values from 0 to 2, as said below
- block_layout: int32 [2, 8, 12], P(None, 'gy'), may hold values from 0 to 11, as said below
- qkv_weight: bfloat16 [1024, 3072], P(('gx', 'gy')), may hold values from -0.1875 to 0.1875
- out_weight: bfloat16 [1024, 1024], P(('gx', 'gy')), may hold values from -6 to 6
- up_weight: bfloat16 [1024, 4096], P(('gx', 'gy')), may hold values from -0.1875 to 0.1875
- down_weight: bfloat16 [4096, 1024], P(('gx', 'gy')), may hold values from -0.09375 to 0.09375
- attn_gain: bfloat16 [1024], P(('gx', 'gy')), may hold values from 0.5 to 1.5
- attn_shift: bfloat16 [1024], P(('gx', 'gy')), may hold values from -3 to 3
- query_bias: bfloat16 [1024], P(('gx', 'gy')), may hold values from -3 to 3
- value_bias: bfloat16 [1024], P(('gx', 'gy')), may hold values from -3 to 3
- out_bias: bfloat16 [1024], P(('gx', 'gy')), may hold values from -3 to 3
- attn_scale: bfloat16 [1024], P(('gx', 'gy')), may hold values from 0.5 to 1.5
- mlp_gain: bfloat16 [1024], P(('gx', 'gy')), may hold values from 0.5 to 1.5
- mlp_shift: bfloat16 [1024], P(('gx', 'gy')), may hold values from -3 to 3
- up_bias: bfloat16 [4096], P(('gx', 'gy')), may hold values from -3 to 3
- down_bias: bfloat16 [1024], P(('gx', 'gy')), may hold values from -3 to 3
- mlp_scale: bfloat16 [1024], P(('gx', 'gy')), may hold values from 0.5 to 1.5
Outputs:
- block_out: bfloat16 [2, 12288, 1024], P(None, ('gx', 'gy'))
- token_grad: bfloat16 [2, 12288, 1024], P(None, ('gx', 'gy'))
- qkv_weight_grad: float32 [1024, 3072], P(('gx', 'gy'))
- out_weight_grad: float32 [1024, 1024], P(('gx', 'gy'))
- up_weight_grad: float32 [1024, 4096], P(('gx', 'gy'))
- down_weight_grad: float32 [4096, 1024], P(('gx', 'gy'))
- attn_gain_grad: float32 [1024], P(('gx', 'gy'))
- attn_shift_grad: float32 [1024], P(('gx', 'gy'))
- query_bias_grad: float32 [1024], P(('gx', 'gy'))
- value_bias_grad: float32 [1024], P(('gx', 'gy'))
- out_bias_grad: float32 [1024], P(('gx', 'gy'))
- attn_scale_grad: float32 [1024], P(('gx', 'gy'))
- mlp_gain_grad: float32 [1024], P(('gx', 'gy'))
- mlp_shift_grad: float32 [1024], P(('gx', 'gy'))
- up_bias_grad: float32 [4096], P(('gx', 'gy'))
- down_bias_grad: float32 [1024], P(('gx', 'gy'))
- mlp_scale_grad: float32 [1024], P(('gx', 'gy'))
Inputs may be any that keep to these rules, and one draw needn't show every extreme that they name: `image_ids`: along each pack (one micro-batch, one column) ids start at 0, never fall and rise by one at each new image; each image covers 1 to 1370 consecutive positions, image 1 covers exactly 1370, and the last image ends at the pack's end. `block_layout`: entry d * 3 + s of a micro-batch and column is s * 4 + ((d + r) mod 4), with one turn r of 0 to 3 for each micro-batch and column.
All inputs are finite; a program needn't handle non-finite values.
Results may differ from a plain program's by a relative error of at most 0.018.
Values may be sent and summed in bfloat16 or wider, within the bound.
A program may use at most 448 MiB of HBM per device.

v0:
```python
import jax
import jax.numpy as jnp
from jax import lax
from jax.sharding import PartitionSpec as P

HEADS = 16
HEAD_DIM = 64
BLOCK = 128


EPS = 1e-06
NEG_FILL = -1e30


def norm_parts(rows, gain, shift):
    mean_row = jnp.mean(rows, axis=-1, keepdims=True)
    centered = rows - mean_row
    inv_std = lax.rsqrt(jnp.mean(centered * centered, axis=-1, keepdims=True) + EPS)
    unit_rows = centered * inv_std
    return (unit_rows * gain + shift, unit_rows, inv_std)


def norm_back(grad_out, unit_rows, inv_std, gain):
    scaled = grad_out * gain
    return inv_std * (
        scaled
        - jnp.mean(scaled, axis=-1, keepdims=True)
        - unit_rows * jnp.mean(scaled * unit_rows, axis=-1, keepdims=True)
    )


def heads_view(rows):
    return rows.reshape(rows.shape[0], HEADS, HEAD_DIM)


def flat_view(head_rows):
    return head_rows.reshape(head_rows.shape[0], HEADS * HEAD_DIM)


def outer_sum(left, right):
    return lax.dot_general(
        left, right, (((0,), (0,)), ((), ())), preferred_element_type=jnp.float32
    )


def back_dot(grad_rows, weight):
    return lax.dot_general(
        grad_rows, weight, (((1,), (1,)), ((), ())), preferred_element_type=jnp.float32
    )


def masked_scores(query_rows, key_rows, query_ids, key_ids):
    raw_scores = jnp.einsum(
        "qhd,khd->hqk",
        heads_view(query_rows),
        heads_view(key_rows),
        preferred_element_type=jnp.float32,
    ) * HEAD_DIM ** (-0.5)
    same_image = query_ids[:, None] == key_ids[None, :]
    return jnp.where(same_image[None], raw_scores, -jnp.inf)


def score_grads(scores, lse_rows, delta_rows, grad_out, value_rows):
    probs = jnp.exp(scores - lse_rows[..., None])
    grad_probs = jnp.einsum(
        "qhd,khd->hqk",
        heads_view(grad_out),
        heads_view(value_rows),
        preferred_element_type=jnp.float32,
    )
    grad_scores = (probs * (grad_probs - delta_rows[..., None])).astype(jnp.bfloat16)
    return (probs.astype(jnp.bfloat16), grad_scores)


def gelu_exact(values):
    return jax.nn.gelu(values, approximate=False)


def attend(query_rows, key_rows, value_rows, own_ids, column_ids):
    row_count = query_rows.shape[0]
    run_max = jnp.full((HEADS, row_count), NEG_FILL, jnp.float32)
    key_piece = lax.all_gather(key_rows, "gx", axis=0, tiled=True)
    value_piece = lax.all_gather(value_rows, "gx", axis=0, tiled=True)
    scores = masked_scores(query_rows, key_piece, own_ids, column_ids)
    new_max = jnp.maximum(run_max, jnp.max(scores, axis=-1))
    weights = jnp.exp(scores - new_max[..., None])
    run_sum = jnp.sum(weights, axis=-1)
    weighted = jnp.einsum(
        "hqk,khd->hqd",
        weights.astype(jnp.bfloat16),
        heads_view(value_piece),
        preferred_element_type=jnp.float32,
    )
    run_max, run_sum, weighted = (new_max, run_sum, weighted)
    out_heads = jnp.transpose(weighted / run_sum[..., None], (1, 0, 2))
    return (flat_view(out_heads), run_max + jnp.log(run_sum))


def attend_back(
    query_rows, key_rows, value_rows, grad_mixed, mixed_full, lse_rows, own_ids, column_ids
):
    score_scale = HEAD_DIM ** (-0.5)
    delta_rows = jnp.transpose(
        jnp.sum(heads_view(grad_mixed.astype(jnp.float32)) * heads_view(mixed_full), axis=-1)
    )
    key_piece = lax.all_gather(key_rows, "gx", axis=0, tiled=True)
    value_piece = lax.all_gather(value_rows, "gx", axis=0, tiled=True)
    scores = masked_scores(query_rows, key_piece, own_ids, column_ids)
    probs_low, grad_scores = score_grads(scores, lse_rows, delta_rows, grad_mixed, value_piece)
    grad_query = score_scale * jnp.einsum(
        "hqk,khd->qhd", grad_scores, heads_view(key_piece), preferred_element_type=jnp.float32
    )
    key_part = score_scale * jnp.einsum(
        "hqk,qhd->khd", grad_scores, heads_view(query_rows), preferred_element_type=jnp.float32
    )
    value_part = jnp.einsum(
        "hqk,qhd->khd", probs_low, heads_view(grad_mixed), preferred_element_type=jnp.float32
    )
    grad_query, grad_keys, grad_values = (grad_query, key_part, value_part)
    grad_keys, grad_values = (
        lax.psum_scatter(
            grad_keys.astype(jnp.bfloat16), "gx", scatter_dimension=0, tiled=True
        ).astype(jnp.float32),
        lax.psum_scatter(
            grad_values.astype(jnp.bfloat16), "gx", scatter_dimension=0, tiled=True
        ).astype(jnp.float32),
    )
    return (flat_view(grad_query), flat_view(grad_keys), flat_view(grad_values))


def shards(
    tokens,
    cotangent,
    image_ids,
    block_layout,
    qkv_weight,
    out_weight,
    up_weight,
    down_weight,
    attn_gain,
    attn_shift,
    query_bias,
    value_bias,
    out_bias,
    attn_scale,
    mlp_gain,
    mlp_shift,
    up_bias,
    down_bias,
    mlp_scale,
):
    param_shards = (
        qkv_weight,
        out_weight,
        up_weight,
        down_weight,
        attn_gain,
        attn_shift,
        query_bias,
        value_bias,
        out_bias,
        attn_scale,
        mlp_gain,
        mlp_shift,
        up_bias,
        down_bias,
        mlp_scale,
    )

    def fetch_params():
        return (
            lax.all_gather(qkv_weight, ("gx", "gy"), axis=0, tiled=True),
            lax.all_gather(out_weight, ("gx", "gy"), axis=0, tiled=True),
            lax.all_gather(up_weight, ("gx", "gy"), axis=0, tiled=True),
            lax.all_gather(down_weight, ("gx", "gy"), axis=0, tiled=True),
            lax.all_gather(attn_gain, ("gx", "gy"), axis=0, tiled=True),
            lax.all_gather(attn_shift, ("gx", "gy"), axis=0, tiled=True),
            lax.all_gather(query_bias, ("gx", "gy"), axis=0, tiled=True),
            lax.all_gather(value_bias, ("gx", "gy"), axis=0, tiled=True),
            lax.all_gather(out_bias, ("gx", "gy"), axis=0, tiled=True),
            lax.all_gather(attn_scale, ("gx", "gy"), axis=0, tiled=True),
            lax.all_gather(mlp_gain, ("gx", "gy"), axis=0, tiled=True),
            lax.all_gather(mlp_shift, ("gx", "gy"), axis=0, tiled=True),
            lax.all_gather(up_bias, ("gx", "gy"), axis=0, tiled=True),
            lax.all_gather(down_bias, ("gx", "gy"), axis=0, tiled=True),
            lax.all_gather(mlp_scale, ("gx", "gy"), axis=0, tiled=True),
        )

    micro_count, row_count, width = tokens.shape
    column_index = lax.axis_index("gx")
    whole_count = lax.axis_size(("gx", "gy"))
    totals = [
        jnp.zeros((shard.shape[0] * whole_count,) + shard.shape[1:], jnp.float32)
        for shard in param_shards
    ]
    outputs = []
    input_grads = []
    for micro_index in range(micro_count):
        fetched = fetch_params()
        qkv_w, out_w, up_w, down_w = (fetched[0], fetched[1], fetched[2], fetched[3])
        (
            gain_attn,
            shift_attn,
            bias_query,
            bias_value,
            bias_out,
            scale_attn,
            gain_mlp,
            shift_mlp,
            bias_up,
            bias_down,
            scale_mlp,
        ) = tuple((vector.astype(jnp.float32) for vector in fetched[4:]))
        layout_row = block_layout[micro_index, 0]
        positions = (
            layout_row[:, None] * BLOCK + jnp.arange(BLOCK, dtype=jnp.int32)[None, :]
        ).reshape(-1)
        column_ids = jnp.take(image_ids[micro_index, 0], positions)
        own_ids = lax.dynamic_slice_in_dim(column_ids, column_index * row_count, row_count)
        x_rows = tokens[micro_index].astype(jnp.float32)
        normed_one, unit_one, inv_one = norm_parts(x_rows, gain_attn, shift_attn)
        normed_one_low = normed_one.astype(jnp.bfloat16)
        projected = jnp.dot(normed_one_low, qkv_w, preferred_element_type=jnp.float32)
        query_rows = (projected[:, :width] + bias_query).astype(jnp.bfloat16)
        key_rows = projected[:, width : 2 * width].astype(jnp.bfloat16)
        value_rows = (projected[:, 2 * width :] + bias_value).astype(jnp.bfloat16)
        mixed_full, lse_rows = attend(query_rows, key_rows, value_rows, own_ids, column_ids)
        mixed_low = mixed_full.astype(jnp.bfloat16)
        branch_one = jnp.dot(mixed_low, out_w, preferred_element_type=jnp.float32) + bias_out
        resid = x_rows + scale_attn * branch_one
        normed_two, unit_two, inv_two = norm_parts(resid, gain_mlp, shift_mlp)
        normed_two_low = normed_two.astype(jnp.bfloat16)
        hidden = jnp.dot(normed_two_low, up_w, preferred_element_type=jnp.float32) + bias_up
        active_low = gelu_exact(hidden).astype(jnp.bfloat16)
        branch_two = jnp.dot(active_low, down_w, preferred_element_type=jnp.float32) + bias_down
        outputs.append((resid + scale_mlp * branch_two).astype(jnp.bfloat16))
        fetched = fetch_params()
        qkv_w, out_w, up_w, down_w = (fetched[0], fetched[1], fetched[2], fetched[3])
        grad_y = cotangent[micro_index].astype(jnp.float32)
        totals[14] = totals[14] + jnp.sum(grad_y * branch_two, axis=0)
        grad_two = (scale_mlp * grad_y).astype(jnp.bfloat16)
        totals[13] = totals[13] + jnp.sum(grad_two.astype(jnp.float32), axis=0)
        totals[3] = totals[3] + outer_sum(active_low, grad_two)
        grad_active = back_dot(grad_two, down_w)
        _, gelu_pull = jax.vjp(gelu_exact, hidden)
        grad_hidden = gelu_pull(grad_active)[0].astype(jnp.bfloat16)
        totals[12] = totals[12] + jnp.sum(grad_hidden.astype(jnp.float32), axis=0)
        totals[2] = totals[2] + outer_sum(normed_two_low, grad_hidden)
        grad_norm_two = back_dot(grad_hidden, up_w)
        totals[10] = totals[10] + jnp.sum(grad_norm_two * unit_two, axis=0)
        totals[11] = totals[11] + jnp.sum(grad_norm_two, axis=0)
        grad_resid = grad_y + norm_back(grad_norm_two, unit_two, inv_two, gain_mlp)
        totals[9] = totals[9] + jnp.sum(grad_resid * branch_one, axis=0)
        grad_one = (scale_attn * grad_resid).astype(jnp.bfloat16)
        totals[8] = totals[8] + jnp.sum(grad_one.astype(jnp.float32), axis=0)
        totals[1] = totals[1] + outer_sum(mixed_low, grad_one)
        grad_mixed = back_dot(grad_one, out_w).astype(jnp.bfloat16)
        grad_query, grad_keys, grad_values = attend_back(
            query_rows, key_rows, value_rows, grad_mixed, mixed_full, lse_rows, own_ids, column_ids
        )
        grad_qkv = jnp.concatenate([grad_query, grad_keys, grad_values], axis=1).astype(
            jnp.bfloat16
        )
        totals[6] = totals[6] + jnp.sum(grad_qkv[:, :width].astype(jnp.float32), axis=0)
        totals[7] = totals[7] + jnp.sum(grad_qkv[:, 2 * width :].astype(jnp.float32), axis=0)
        totals[0] = totals[0] + outer_sum(normed_one_low, grad_qkv)
        grad_norm_one = back_dot(grad_qkv, qkv_w)
        totals[4] = totals[4] + jnp.sum(grad_norm_one * unit_one, axis=0)
        totals[5] = totals[5] + jnp.sum(grad_norm_one, axis=0)
        grad_x = grad_resid + norm_back(grad_norm_one, unit_one, inv_one, gain_attn)
        input_grads.append(grad_x.astype(jnp.bfloat16))
    reduced = (
        lax.psum_scatter(totals[0], ("gx", "gy"), scatter_dimension=0, tiled=True),
        lax.psum_scatter(totals[1], ("gx", "gy"), scatter_dimension=0, tiled=True),
        lax.psum_scatter(totals[2], ("gx", "gy"), scatter_dimension=0, tiled=True),
        lax.psum_scatter(totals[3], ("gx", "gy"), scatter_dimension=0, tiled=True),
        lax.psum_scatter(totals[4], ("gx", "gy"), scatter_dimension=0, tiled=True),
        lax.psum_scatter(totals[5], ("gx", "gy"), scatter_dimension=0, tiled=True),
        lax.psum_scatter(totals[6], ("gx", "gy"), scatter_dimension=0, tiled=True),
        lax.psum_scatter(totals[7], ("gx", "gy"), scatter_dimension=0, tiled=True),
        lax.psum_scatter(totals[8], ("gx", "gy"), scatter_dimension=0, tiled=True),
        lax.psum_scatter(totals[9], ("gx", "gy"), scatter_dimension=0, tiled=True),
        lax.psum_scatter(totals[10], ("gx", "gy"), scatter_dimension=0, tiled=True),
        lax.psum_scatter(totals[11], ("gx", "gy"), scatter_dimension=0, tiled=True),
        lax.psum_scatter(totals[12], ("gx", "gy"), scatter_dimension=0, tiled=True),
        lax.psum_scatter(totals[13], ("gx", "gy"), scatter_dimension=0, tiled=True),
        lax.psum_scatter(totals[14], ("gx", "gy"), scatter_dimension=0, tiled=True),
    )
    return (jnp.stack(outputs), jnp.stack(input_grads)) + tuple(reduced)


def solution(mesh):
    return jax.shard_map(
        shards,
        mesh=mesh,
        in_specs=(
            P(None, ("gx", "gy"), None),
            P(None, ("gx", "gy"), None),
            P(None, "gy", None),
            P(None, "gy", None),
            P(("gx", "gy"), None),
            P(("gx", "gy"), None),
            P(("gx", "gy"), None),
            P(("gx", "gy"), None),
            P(("gx", "gy")),
            P(("gx", "gy")),
            P(("gx", "gy")),
            P(("gx", "gy")),
            P(("gx", "gy")),
            P(("gx", "gy")),
            P(("gx", "gy")),
            P(("gx", "gy")),
            P(("gx", "gy")),
            P(("gx", "gy")),
            P(("gx", "gy")),
        ),
        out_specs=(
            P(None, ("gx", "gy"), None),
            P(None, ("gx", "gy"), None),
            P(("gx", "gy"), None),
            P(("gx", "gy"), None),
            P(("gx", "gy"), None),
            P(("gx", "gy"), None),
            P(("gx", "gy")),
            P(("gx", "gy")),
            P(("gx", "gy")),
            P(("gx", "gy")),
            P(("gx", "gy")),
            P(("gx", "gy")),
            P(("gx", "gy")),
            P(("gx", "gy")),
            P(("gx", "gy")),
            P(("gx", "gy")),
            P(("gx", "gy")),
        ),
        check_vma=False,
    )
```

profile of v0, /device:TPU:0, one launch (start us, length us, event | category | flops | bytes accessed | tf_op | source)
XLA Modules:
  0.0 1574.7 jit_solution(17283277379549753197)
XLA Ops:
  16.4 42.7 %all-reduce.22 = (bf16[1024]{0:T(1024)(128)(2,1)S(1)}, bf16[1024]{0:T(1024)(128)(2,1)S(1)}, bf16[1024]{0:T(1024)(128)(2,1)S(1)}, bf16[1024]{0:T(1024)(128)(2,1)S...) all-reduce(bf16[1024]{0:T(1024)(128)(2,1)S(1)} %dynamic-update-slic, ...), channel_id=1, replica_groups=mesh['gx'=4,'gy'=8] {'gx','gy'}, use_global_device_ids=true, to_apply=%add.2 | all-reduce | flops 10240 | bytes 40960
  62.7 20.5 %all-gather.10.cloned.1.call-done = bf16[1024,3072]{1,0:T(8,128)(2,1)} async-done(((bf16[32,3072]{1,0:T(8,128)(2,1)}), bf16[1024,3072]{1,0:T(8,128)(2,1)}) %all-gather.10.cloned.1.call-update) | async-done | bytes 6291472 | tf_op jit(solution)/shard_map/all_gather | solution.py:172
  127.1 39.6 %all-gather = bf16[32,1,128]{2,1,0:T(2,128)(2,1)S(1)} all-gather(bf16[1,1,128]{2,1,0:T(2,128)(2,1)S(1)} %bitcast.274), channel_id=1, replica_groups=mesh['gx'=4,'gy'=8] {'gx','gy'}, dimensions={0}, use_global_device_ids=true | all-gather | bytes 8448 | tf_op jit(solution)/shard_map/all_gather | solution.py:184
  191.2 26.2 %all-gather.22.cloned.1.call-done = bf16[1536,1024]{1,0:T(8,128)(2,1)} async-done(((bf16[384,1024]{1,0:T(8,128)(2,1)}), bf16[1536,1024]{1,0:T(8,128)(2,1)}) %all-gather.22.cloned.1.call-update) | async-done | bytes 3145744 | tf_op jit(solution)/shard_map/all_gather | solution.py:82
  220.6 17.7 %fusion.7 = (f32[16,384]{1,0:T(8,128)S(1)}, f32[16,384,1536]{2,1,0:T(8,128)}) fusion(pred[384,1536]{1,0:T(8,128)(4,1)} %broadcast_compare_fusion, bf16[384,16,64]{0,2,1:T(8,128)(2,1)} %bitcast.246, bf16[1536,16,64]{0,2,1:T(8,128)(2,1)S(1)} %bitcast.242), kind=kOutput, calls=%fused_computation.17 | convolution fusion | flops 1236264960 | bytes 42295296 | tf_op jit(solution)/shard_map/qhd,khd->hqk/dot_general | solution.py:53
  255.8 25.7 %all-gather.24.cloned.1.call-done = bf16[1536,1024]{1,0:T(8,128)(2,1)} async-done(((bf16[384,1024]{1,0:T(8,128)(2,1)}), bf16[1536,1024]{1,0:T(8,128)(2,1)}) %all-gather.24.cloned.1.call-update) | async-done | bytes 3145744 | tf_op jit(solution)/shard_map/all_gather | solution.py:83
  286.2 19.0 %fusion.128 = (bf16[384,16,64]{0,2,1:T(8,128)(2,1)}, f32[384,16,64]{0,2,1:T(8,128)}) fusion(f32[384,16]{0,1:T(8,128)S(1)} %bitcast.268, bf16[1536,16,64]{0,2,1:T(8,128)(2,1)} %bitcast.258, f32[16,384,1536]{2,1,0:T(8,128)} %get-tuple-element.112, f32[16,384]{1,0:T(8,128)S(1)} %broadcast_maximum_fusion, pred[384,1536]{1,0:T(8,128)(4,1)S(1)} %copy-done.21), kind=kOutput, calls=%fused_computation.232 | convolution fusion | flops 1246494720 | bytes 43892736 | tf_op jit(solution)/shard_map/hqk,khd->hqd/dot_general | solution.py:88
  322.5 23.2 %all-gather.14.cloned.1.call-done = bf16[1536,1024]{1,0:T(8,128)(2,1)} async-done(((bf16[384,1024]{1,0:T(8,128)(2,1)}), bf16[1536,1024]{1,0:T(8,128)(2,1)}) %all-gather.14.cloned.1.call-update) | async-done | bytes 3145744 | tf_op jit(solution)/shard_map/all_gather | solution.py:83
  350.4 53.1 %all-gather.16.cloned.1.call-done = bf16[1024,1024]{1,0:T(8,128)(2,1)} async-done(((bf16[32,1024]{1,0:T(8,128)(2,1)}), bf16[1024,1024]{1,0:T(8,128)(2,1)}) %all-gather.16.cloned.1.call-update) | async-done | bytes 2097168 | tf_op jit(solution)/shard_map/all_gather | solution.py:173
  406.4 18.6 %fusion.127 = (bf16[384,16,64]{0,2,1:T(8,128)(2,1)S(1)}, f32[384,16,64]{0,2,1:T(8,128)}) fusion(f32[384,16]{0,1:T(8,128)S(1)} %bitcast.269, bf16[1536,16,64]{0,2,1:T(8,128)(2,1)} %bitcast.260, f32[16,384,1536]{2,1,0:T(8,128)} %get-tuple-element.108, f32[16,384]{1,0:T(8,128)S(1)} %broadcast_maximum_fusion.1, pred[384,1536]{1,0:T(8,128)(4,1)S(1)} %copy-done.24), kind=kOutput, calls=%fused_computation.231 | convolution fusion | flops 1246494720 | bytes 43892736 | tf_op jit(solution)/shard_map/hqk,khd->hqd/dot_general | solution.py:88
  429.3 53.2 %all-gather.18.cloned.1.call-done = bf16[1024,4096]{1,0:T(8,128)(2,1)} async-done(((bf16[32,4096]{1,0:T(8,128)(2,1)}), bf16[1024,4096]{1,0:T(8,128)(2,1)}) %all-gather.18.cloned.1.call-update) | async-done | bytes 8388624 | tf_op jit(solution)/shard_map/all_gather | solution.py:174
  482.5 21.1 %multiply_convert_fusion.5 = (bf16[384,4096]{1,0:T(8,128)(2,1)}, f32[384,4096]{1,0:T(8,128)}, f32[384,4096]{1,0:T(8,128)}) fusion(f32[4096]{0:T(1024)S(1)} %bitcast.272, bf16[1024,4096]{1,0:T(8,128)(2,1)} %all-gather.18.cloned.1.call-done, f32[384,1024]{1,0:T(8,128)} %copy-done.10, f32[1024]{0:T(1024)S(1)} %convert_element_type.244, ...), kind=kOutput, calls=%fused_computation.52 | convolution fusion | flops 3327000576 | bytes 25717760 | tf_op jit(solution)/shard_map/dot_general | solution.py:233
  503.6 21.1 %multiply_convert_fusion.4 = (bf16[384,4096]{1,0:T(8,128)(2,1)}, f32[384,4096]{1,0:T(8,128)}, f32[384,4096]{1,0:T(8,128)}) fusion(f32[4096]{0:T(1024)S(1)} %bitcast.273, bf16[1024,4096]{1,0:T(8,128)(2,1)S(1)} %copy-done.109, f32[384,1024]{1,0:T(8,128)S(1)} %get-tuple-element.96, f32[384]{0:T(512)S(1)} %add_rsqrt_fusion, ...), kind=kOutput, calls=%fused_computation.39 | convolution fusion | flops 3327000576 | bytes 25717760 | tf_op jit(solution)/shard_map/dot_general | solution.py:233
  524.7 36.7 %all-gather.20.cloned.1.call-done = bf16[4096,1024]{1,0:T(8,128)(2,1)} async-done(((bf16[128,1024]{1,0:T(8,128)(2,1)}), bf16[4096,1024]{1,0:T(8,128)(2,1)}) %all-gather.20.cloned.1.call-update) | async-done | bytes 8388624 | tf_op jit(solution)/shard_map/all_gather | solution.py:175
  623.3 18.6 %fusion.32 = bf16[16,64,1536]{2,1,0:T(8,128)(2,1)} fusion(bf16[384,16,64]{0,2,1:T(8,128)(2,1)} %bitcast.266, f32[16,384,1536]{2,1,0:T(8,128)} %get-tuple-element.108, f32[16,384]{1,0:T(8,128)S(1)} %log_add_fusion.1, pred[384,1536]{1,0:T(8,128)(4,1)S(1)} %copy-done.25), kind=kOutput, calls=%fused_computation.69 | convolution fusion | flops 1247281152 | bytes 42295296 | tf_op jit(solution)/shard_map/hqk,qhd->khd/dot_general | solution.py:116
  651.4 18.8 %fusion.35 = bf16[16,64,1536]{2,1,0:T(8,128)(2,1)} fusion(bf16[384,16,64]{0,2,1:T(8,128)(2,1)S(1)} %bitcast.264, f32[16,384,1536]{2,1,0:T(8,128)} %get-tuple-element.112, f32[16,384]{1,0:T(8,128)S(1)} %log_add_fusion, pred[384,1536]{1,0:T(8,128)(4,1)S(1)} %copy-done.22), kind=kOutput, calls=%fused_computation.70 | convolution fusion | flops 1247281152 | bytes 42295296 | tf_op jit(solution)/shard_map/hqk,qhd->khd/dot_general | solution.py:116
  676.9 26.7 %multiply_convert_fusion.1 = bf16[16,384,1536]{2,1,0:T(8,128)(2,1)} fusion(f32[16,384,1536]{2,1,0:T(8,128)} %get-tuple-element.108, f32[16,384]{1,0:T(8,128)S(1)} %bitcast.270, f32[16,384]{1,0:T(8,128)S(1)} %copy-done.88, pred[384,1536]{1,0:T(8,128)(4,1)S(1)} %copy-done.25, bf16[384,16,64]{0,2,1:T(8,128)(2,1)S(1)} %bitcast.267, ...), kind=kOutput, calls=%fused_computation.4 | convolution fusion | flops 1264582656 | bytes 61194240 | tf_op jit(solution)/shard_map/qhd,khd->hqk/dot_general | solution.py:65
  718.5 26.7 %multiply_convert_fusion = bf16[16,384,1536]{2,1,0:T(8,128)(2,1)} fusion(f32[16,384,1536]{2,1,0:T(8,128)} %get-tuple-element.112, f32[16,384]{1,0:T(8,128)S(1)} %bitcast.271, f32[16,384]{1,0:T(8,128)S(1)} %copy-done.90, pred[384,1536]{1,0:T(8,128)(4,1)S(1)} %copy-done.23, bf16[384,16,64]{0,2,1:T(8,128)(2,1)S(1)} %bitcast.265, bf16[1536,16,64]{0,2,1:T(8,128)(2,1)} %bitcast.259), kind=kOutput, calls=%fused_computation.2 | convolution fusion | flops 1264582656 | bytes 61194240 | tf_op jit(solution)/shard_map/qhd,khd->hqk/dot_general | solution.py:65
  792.0 38.8 %reduce-scatter.25.cloned.1.call-done = bf16[384,1024]{1,0:T(8,128)(2,1)} async-done(((bf16[1536,1024]{1,0:T(8,128)(2,1)}), bf16[384,1024]{1,0:T(8,128)(2,1)}) %reduce-scatter.25.cloned.1.call-update) | async-done | bytes 786448
  833.1 60.1 %reduce-scatter.29.cloned.1.call-done = bf16[384,1024]{1,0:T(8,128)(2,1)} async-done(((bf16[1536,1024]{1,0:T(8,128)(2,1)}), bf16[384,1024]{1,0:T(8,128)(2,1)}) %reduce-scatter.29.cloned.1.call-update) | async-done | bytes 786448
  970.4 42.0 %all-reduce.21 = (f32[1024]{0:T(1024)S(1)}, f32[1024]{0:T(1024)S(1)}, f32[1024]{0:T(1024)S(1)}, f32[1024]{0:T(1024)S(1)}, f32[1024]{0:T(1024)S(1)}, /*index=5*/f...) all-reduce(f32[1024]{0:T(1024)S(1)} %add.343, ...), channel_id=10, replica_groups=mesh['gx'=4,'gy'=8] {'gx','gy'}, use_global_device_ids=true, to_apply=%region_32.34.clone | all-reduce | flops 14336 | bytes 114688
  1037.6 158.1 %reduce-scatter.17.cloned.1.call-done = f32[32,3072]{1,0:T(8,128)} async-done(((f32[1024,3072]{1,0:T(8,128)}), f32[32,3072]{1,0:T(8,128)}) %reduce-scatter.17.cloned.1.call-update) | async-done | bytes 393232 | tf_op jit(solution)/shard_map/reduce_scatter | solution.py:273
  1195.7 184.9 %reduce-scatter.23.cloned.1.call-done = f32[128,1024]{1,0:T(8,128)} async-done(((f32[4096,1024]{1,0:T(8,128)}), f32[128,1024]{1,0:T(8,128)}) %reduce-scatter.23.cloned.1.call-update) | async-done | bytes 524304 | tf_op jit(solution)/shard_map/reduce_scatter | solution.py:276
  1380.6 187.4 %reduce-scatter.21.cloned.1.call-done = f32[32,4096]{1,0:T(8,128)} async-done(((f32[1024,4096]{1,0:T(8,128)}), f32[32,4096]{1,0:T(8,128)}) %reduce-scatter.21.cloned.1.call-update) | async-done | bytes 524304 | tf_op jit(solution)/shard_map/reduce_scatter | solution.py:275
  (416 shorter events, 378.4 us)
Async XLA Ops:
  7.2 76.1 %all-gather.10.cloned.1.call-start = ((), (), s32[]{:S(2)}) async-start(), calls=%async_computation.8 | async-start | bytes 6488064 | tf_op jit(solution)/shard_map/all_gather | solution.py:172
  7.9 162.3 %all-gather.12.cloned.1.call-start = ((), (), s32[]{:S(2)}) async-start(), calls=%async_computation.9 | async-start | bytes 3932160 | tf_op jit(solution)/shard_map/all_gather | solution.py:82
  91.4 126.0 %all-gather.22.cloned.1.call-start = ((), (), s32[]{:S(2)}) async-start(), calls=%async_computation.14 | async-start | bytes 3932160 | tf_op jit(solution)/shard_map/all_gather | solution.py:82
  99.6 181.9 %all-gather.24.cloned.1.call-start = ((), (), s32[]{:S(2)}) async-start(), calls=%async_computation.15 | async-start | bytes 3932160 | tf_op jit(solution)/shard_map/all_gather | solution.py:83
  104.6 241.1 %all-gather.14.cloned.1.call-start = ((), (), s32[]{:S(2)}) async-start(), calls=%async_computation.10 | async-start | bytes 3932160 | tf_op jit(solution)/shard_map/all_gather | solution.py:83
  105.2 298.3 %all-gather.16.cloned.1.call-start = ((), (), s32[]{:S(2)}) async-start(), calls=%async_computation.11 | async-start | bytes 2162688 | tf_op jit(solution)/shard_map/all_gather | solution.py:173
  105.8 376.7 %all-gather.18.cloned.1.call-start = ((), (), s32[]{:S(2)}) async-start(), calls=%async_computation.12 | async-start | bytes 8650752 | tf_op jit(solution)/shard_map/all_gather | solution.py:174
  106.6 454.9 %all-gather.20.cloned.1.call-start = ((), (), s32[]{:S(2)}) async-start(), calls=%async_computation.13 | async-start | bytes 8650752 | tf_op jit(solution)/shard_map/all_gather | solution.py:175
  107.3 679.8 %reduce-scatter.27.cloned.1.call-start = ((), (), s32[]{:S(2)}) async-start(), calls=%async_computation.21 | async-start | bytes 3932160
  127.1 482.7 %copy-start.57 = (f32[1024]{0:T(1024)}, f32[1024]{0:T(1024)S(1)}, u32[]{:S(2)}) copy-start(f32[1024]{0:T(1024)S(1)} %convert_element_type.243) | copy-start | bytes 12292
  127.1 376.5 %copy-start.63 = (f32[1024]{0:T(1024)}, f32[1024]{0:T(1024)S(1)}, u32[]{:S(2)}) copy-start(f32[1024]{0:T(1024)S(1)} %convert_element_type.244) | copy-start | bytes 12292
  427.4 182.3 %copy-start.8 = (f32[384,1024]{1,0:T(8,128)}, f32[384,1024]{1,0:T(8,128)S(1)}, u32[]{:S(2)}) copy-start(f32[384,1024]{1,0:T(8,128)S(1)} %get-tuple-element.96) | copy-start | bytes 4718596
  427.4 182.3 %copy-start.73 = (f32[384]{0:T(512)}, f32[384]{0:T(512)S(1)}, u32[]{:S(2)}) copy-start(f32[384]{0:T(512)S(1)} %broadcast_multiply_fusion.10) | copy-start | bytes 4612
  428.9 172.2 %copy-start.75 = (f32[384]{0:T(512)}, f32[384]{0:T(512)S(1)}, u32[]{:S(2)}) copy-start(f32[384]{0:T(512)S(1)} %broadcast_multiply_fusion.8) | copy-start | bytes 4612
  429.3 180.5 %copy-start.77 = (f32[384]{0:T(512)}, f32[384]{0:T(512)S(1)}, u32[]{:S(2)}) copy-start(f32[384]{0:T(512)S(1)} %add_rsqrt_fusion.2) | copy-start | bytes 4612
  429.3 171.8 %copy-start.85 = (f32[384]{0:T(512)}, f32[384]{0:T(512)S(1)}, u32[]{:S(2)}) copy-start(f32[384]{0:T(512)S(1)} %add_rsqrt_fusion) | copy-start | bytes 4612
  429.3 194.0 %copy-start.87 = (f32[16,384]{1,0:T(8,128)}, f32[16,384]{1,0:T(8,128)S(1)}, u32[]{:S(2)}) copy-start(f32[16,384]{1,0:T(8,128)S(1)} %log_add_fusion.1) | copy-start | bytes 73732
  646.7 143.1 %reduce-scatter.31.cloned.1.call-start = ((), (), s32[]{:S(2)}) async-start(), calls=%async_computation.23 | async-start | bytes 3932160
  675.0 155.8 %reduce-scatter.25.cloned.1.call-start = ((), (), s32[]{:S(2)}) async-start(), calls=%async_computation.20 | async-start | bytes 3932160
  716.7 176.5 %reduce-scatter.29.cloned.1.call-start = ((), (), s32[]{:S(2)}) async-start(), calls=%async_computation.22 | async-start | bytes 3932160
  758.4 279.2 %reduce-scatter.19.cloned.1.call-start = ((), (), s32[]{:S(2)}) async-start(), calls=%async_computation.17 | async-start | bytes 4325376 | tf_op jit(solution)/shard_map/reduce_scatter | solution.py:274
  764.3 431.4 %reduce-scatter.17.cloned.1.call-start = ((), (), s32[]{:S(2)}) async-start(), calls=%async_computation.16 | async-start | bytes 12976128 | tf_op jit(solution)/shard_map/reduce_scatter | solution.py:273
  910.4 470.1 %reduce-scatter.23.cloned.1.call-start = ((), (), s32[]{:S(2)}) async-start(), calls=%async_computation.19 | async-start | bytes 17301504 | tf_op jit(solution)/shard_map/reduce_scatter | solution.py:276
  930.6 637.3 %reduce-scatter.21.cloned.1.call-start = ((), (), s32[]{:S(2)}) async-start(), calls=%async_computation.18 | async-start | bytes 17301504 | tf_op jit(solution)/shard_map/reduce_scatter | solution.py:275
  (107 other events, 1675.1 us)
Sparse Core Ops, SparseCore 0:
  10.9 72.3 all-gather.9
  91.5 62.1 all-gather.11
  155.2 62.0 all-gather.21
  219.4 62.1 all-gather.23
  283.5 62.1 all-gather.13
  348.4 55.0 all-gather.15
  406.4 76.1 all-gather.17
  485.4 76.0 all-gather.19
  646.8 58.8 reduce-scatter.26
  707.8 60.2 reduce-scatter.30
  770.4 60.2 reduce-scatter.24
  832.9 60.2 reduce-scatter.28
  896.0 141.4 reduce-scatter.18
  1044.0 151.6 reduce-scatter.16
  1198.5 182.0 reduce-scatter.22
  1383.4 184.5 reduce-scatter.20
where the time goes:
time: 1580 us; the launch traced here: 1570 us
  waiting for transfers between devices  886 us (56%)
  matrix products  392 us (25%)
  blocking collectives  124 us (8%)
  local copies, waits for them, and re-layouts  97.4 us (6%)
  other arithmetic  59.1 us (4%)
  between operations  15.8 us (1%)
    reduce_scatter x1, waiting for transfers between devices, shards(): lax.psum_scatter(totals[2], ('gx', 'gy'), scatter_dimension=0, tiled=True)  187 us
    reduce_scatter x1, waiting for transfers between devices, shards(): lax.psum_scatter(totals[3], ('gx', 'gy'), scatter_dimension=0, tiled=True)  185 us
    reduce_scatter x1, waiting for transfers between devices, shards(): lax.psum_scatter(totals[0], ('gx', 'gy'), scatter_dimension=0, tiled=True)  158 us
    unnamed x20, waiting for transfers between devices  102 us
    unnamed x2, blocking collectives  84.6 us
    dot_general x8, matrix products, outer_sum(): lax.dot_general(left, right, (((0,), (0,)), ((), ())), preferred_element_...  61.2 us
    dot_general x8, matrix products, back_dot(): lax.dot_general(grad_rows, weight, (((1,), (1,)), ((), ())), preferred_el...  55.2 us
    dot_general x2, matrix products, score_grads(): jnp.einsum('qhd,khd->hqk', heads_view(grad_out), heads_view(value_rows),...  53.4 us
  transfers between devices with their start and end apart: 16, of which 13 were waited for; matrix products, arithmetic and copies ran while one was open for 28% of the time, Pallas kernels for 0%

commit v1 on v0

v1 whole, which is shorter than its diff:
```python
import functools

import jax
import jax.numpy as jnp
from jax import lax
from jax.experimental import pallas as pl
from jax.experimental.pallas import tpu as pltpu
from jax.sharding import PartitionSpec as P

HEAD_DIM = 64
PAIR = 2 * HEAD_DIM
BLOCK = 128
EPS = 1e-06
MASKED = -1e30
ID_LANES = 8
SCALE = HEAD_DIM ** (-0.5)
LOG2E = 1.4426950408889634
EXP_SCALE = SCALE * LOG2E
AXES = ("gx", "gy")
NT = (((1,), (1,)), ((), ()))
NN = (((1,), (0,)), ((), ()))
VMEM_BYTES = 50 * 1024 * 1024


def dot32(left, right, dims):
    return lax.dot_general(left, right, dims, preferred_element_type=jnp.float32)


def norm_parts(rows, gain, shift):
    mean_row = jnp.mean(rows, axis=-1, keepdims=True)
    centered = rows - mean_row
    inv_std = lax.rsqrt(jnp.mean(centered * centered, axis=-1, keepdims=True) + EPS)
    unit_rows = centered * inv_std
    return (unit_rows * gain + shift, unit_rows, inv_std)


def norm_back(grad_out, unit_rows, inv_std, gain):
    scaled = grad_out * gain
    return inv_std * (
        scaled
        - jnp.mean(scaled, axis=-1, keepdims=True)
        - unit_rows * jnp.mean(scaled * unit_rows, axis=-1, keepdims=True)
    )


def outer_sum(left, right):
    return dot32(left, right, (((0,), (0,)), ((), ())))


def back_dot(grad_rows, weight):
    return dot32(grad_rows, weight, NT)


def lane_of(shape):
    return lax.broadcasted_iota(jnp.int32, shape, len(shape) - 1)


def attend_kernel(group, *refs):
    q_ref, qmask_ref = refs[:2]
    k_refs = refs[2 : 2 + group]
    v_refs = refs[2 + group : 2 + 2 * group]
    mask_refs = refs[2 + 2 * group : 2 + 3 * group]
    out_ref, lse_ref = refs[2 + 3 * group :]
    q = q_ref[...].astype(jnp.float32)
    qmask = qmask_ref[...].astype(jnp.float32)
    first = lane_of(q.shape) < HEAD_DIM
    key_first = lane_of(k_refs[0].shape) < HEAD_DIM
    accs, tops = [], []
    for head in range(2):
        q_head = jnp.where(first == (head == 0), q, qmask).astype(jnp.bfloat16)
        mine = key_first == (head == 0)
        scores = []
        for k_ref, mask_ref in zip(k_refs, mask_refs):
            k_head = jnp.where(
                mine, k_ref[...].astype(jnp.float32), mask_ref[...].astype(jnp.float32)
            ).astype(jnp.bfloat16)
            scores.append(dot32(q_head, k_head, NT))
        top = functools.reduce(
            jnp.maximum, [jnp.max(score, axis=-1, keepdims=True) for score in scores]
        )
        acc = jnp.zeros(q.shape, jnp.float32)
        for score, v_ref in zip(scores, v_refs):
            weights = jnp.exp2((score - top) * EXP_SCALE).astype(jnp.bfloat16)
            v_head = jnp.where(mine, v_ref[...].astype(jnp.float32), 1.0).astype(jnp.bfloat16)
            acc = acc + dot32(weights, v_head, NN)
        accs.append(acc)
        tops.append(top)
    mixed = jnp.where(first, accs[0], accs[1])
    sums = jnp.where(first, accs[1], accs[0])
    out_ref[...] = (mixed / pltpu.roll(sums, HEAD_DIM, 1)).astype(out_ref.dtype)
    lse_ref[...] = jnp.where(first, tops[1], tops[0]) + jnp.log2(sums) * (1.0 / EXP_SCALE)


def attend(qkv_rows, others, query_mask, key_masks):
    rows, width = qkv_rows.shape[0], qkv_rows.shape[1] // 3
    pairs = width // PAIR
    tile = rows // 2
    group = 1 + len(others)

    def col(offset):
        return pl.BlockSpec((rows, PAIR), lambda j, i: (0, offset * pairs + j))

    whole = pl.BlockSpec((rows, PAIR), lambda j, i: (0, 0))
    tiled = pl.BlockSpec((tile, PAIR), lambda j, i: (i, j))
    cells = 2 * pairs * rows * rows * group
    return pl.pallas_call(
        functools.partial(attend_kernel, group),
        grid=(pairs, 2),
        in_specs=[tiled, pl.BlockSpec((tile, PAIR), lambda j, i: (i, 0))]
        + [col(1)]
        + [col(0)] * (group - 1)
        + [col(2)]
        + [col(1)] * (group - 1)
        + [whole] * group,
        out_specs=[tiled, tiled],
        out_shape=[
            jax.ShapeDtypeStruct((rows, width), jnp.bfloat16),
            jax.ShapeDtypeStruct((rows, width), jnp.float32),
        ],
        compiler_params=pltpu.CompilerParams(vmem_limit_bytes=VMEM_BYTES),
        cost_estimate=pl.CostEstimate(
            flops=cells * 512, bytes_accessed=rows * width * 16, transcendentals=cells
        ),
        name="attend",
    )(qkv_rows, query_mask, qkv_rows, *others, qkv_rows, *others, *key_masks)


def back_kernel(has_prior, *refs):
    q_ref, g_ref, o_ref, lse_ref, qmask_ref, k_ref, v_ref, kmask_ref = refs[:8]
    prior_ref = refs[8] if has_prior else None
    dq_ref, dk_ref, dv_ref = refs[8 + has_prior :]
    q_low, g_low, k_low = q_ref[...], g_ref[...], k_ref[...]
    q = q_low.astype(jnp.float32)
    g = g_low.astype(jnp.float32)
    k = k_low.astype(jnp.float32)
    v = v_ref[...].astype(jnp.float32)
    qmask = qmask_ref[...].astype(jnp.float32)
    kmask = kmask_ref[...].astype(jnp.float32)
    lse = lse_ref[...]
    product = g * o_ref[...].astype(jnp.float32)
    lane = lane_of(q.shape)
    first = lane < HEAD_DIM
    spare = lane % HEAD_DIM
    key_lane = lane_of(k.shape)
    key_first = key_lane < HEAD_DIM
    key_spare = key_lane % HEAD_DIM
    ones = (key_spare >= ID_LANES) & (key_spare < ID_LANES + 3)
    key_fill = jnp.where(ones, -1.0, kmask)
    value_fill = jnp.where(ones, -1.0, 0.0)
    k_turned = k.T.astype(jnp.bfloat16)

    def split(values, rest):
        high = values.astype(jnp.bfloat16).astype(jnp.float32)
        left = values - high
        middle = left.astype(jnp.bfloat16).astype(jnp.float32)
        low = left - middle
        return jnp.where(
            spare == ID_LANES,
            high,
            jnp.where(
                spare == ID_LANES + 1, middle, jnp.where(spare == ID_LANES + 2, low, rest)
            ),
        )

    query_fill = split(lse, qmask)
    delta = [
        jnp.sum(jnp.where(first == (head == 0), product, 0.0), axis=-1, keepdims=True)
        for head in range(2)
    ]
    grad_fill = split(jnp.where(first, delta[1], delta[0]), 0.0)
    dq_turned, dks, dvs = [], [], []
    for head in range(2):
        mine = first == (head == 0)
        key_mine = key_first == (head == 0)
        q_head = jnp.where(mine, q, query_fill).astype(jnp.bfloat16)
        g_head = jnp.where(mine, g, grad_fill).astype(jnp.bfloat16)
        k_head = jnp.where(key_mine, k, key_fill).astype(jnp.bfloat16)
        v_head = jnp.where(key_mine, v, value_fill).astype(jnp.bfloat16)
        probs = jnp.exp2(dot32(k_head, q_head, NT) * EXP_SCALE)
        grads = (probs * dot32(v_head, g_head, NT)).astype(jnp.bfloat16)
        dvs.append(dot32(probs.astype(jnp.bfloat16), g_low, NN))
        dks.append(dot32(grads, q_low, NN))
        dq_turned.append(
            dot32(k_turned[head * HEAD_DIM : (head + 1) * HEAD_DIM], grads, NN)
        )
    dq = jnp.concatenate(dq_turned, axis=0).T * SCALE
    if has_prior:
        dq = dq + prior_ref[...]
    dq_ref[...] = dq.astype(dq_ref.dtype)
    dk_ref[...] = (jnp.where(key_first, dks[0], dks[1]) * SCALE).astype(dk_ref.dtype)
    dv_ref[...] = jnp.where(key_first, dvs[0], dvs[1]).astype(dv_ref.dtype)


def attend_back(
    qkv_rows, grad_mixed, mixed, lse, query_mask, key_value, key_mask, prior, own, last
):
    rows, width = mixed.shape
    pairs = width // PAIR

    def col(offset):
        return pl.BlockSpec((rows, PAIR), lambda j: (0, offset * pairs + j))

    whole = pl.BlockSpec((rows, PAIR), lambda j: (0, 0))
    has_prior = prior is not None
    cells = 2 * pairs * rows * rows
    return pl.pallas_call(
        functools.partial(back_kernel, has_prior),
        grid=(pairs,),
        in_specs=[col(0)] * 4
        + [whole, col(1 if own else 0), col(2 if own else 1), whole]
        + [col(0)] * has_prior,
        out_specs=[col(0)] * 3,
        out_shape=[
            jax.ShapeDtypeStruct((rows, width), jnp.bfloat16 if last else jnp.float32),
            jax.ShapeDtypeStruct((rows, width), jnp.bfloat16),
            jax.ShapeDtypeStruct((rows, width), jnp.bfloat16),
        ],
        compiler_params=pltpu.CompilerParams(vmem_limit_bytes=VMEM_BYTES),
        cost_estimate=pl.CostEstimate(
            flops=cells * 1280, bytes_accessed=rows * width * 20, transcendentals=cells
        ),
        name="attend_back",
    )(
        qkv_rows,
        grad_mixed,
        mixed,
        lse,
        query_mask,
        key_value,
        key_value,
        key_mask,
        *([prior] if has_prior else []),
    )


def gelu_parts(values):
    phi = 0.5 * (1.0 + lax.erf(values * 0.7071067811865476))
    density = 0.3989422804014327 * jnp.exp(-0.5 * values * values)
    return values * phi, phi + values * density


def shards(n_gx, n_gy, tokens, cotangent, image_ids, block_layout, *params):
    qkv_weight, out_weight, up_weight, down_weight = params[:4]
    vectors = params[4:]
    devices = n_gx * n_gy
    chips = n_gx // 4
    group = 2 * chips
    row_count, width = tokens.shape[1:]
    place = lax.axis_index("gx")
    odd = place % 2 == 1

    def linear(line, pack, member):
        return (pack * chips + member // 2) * n_gy + 2 * line + member % 2

    moves = [
        [
            (z * n_gy + 2 * line + core, linear(line, 2 * ((step + z) % 2) + core, z // 2))
            for z in range(n_gx)
            for line in range(n_gy // 2)
            for core in range(2)
        ]
        for step in range(2)
    ]
    rounds = [
        [
            (linear(line, pack, member), linear(line, pack, (member + turn) % group))
            for line in range(n_gy // 2)
            for pack in range(4)
            for member in range(group)
        ]
        for turn in range(1, group)
    ]

    def back(perm):
        return [(target, source) for source, target in perm]

    def to_packs(pair):
        even_first = [jnp.where(odd, pair[1], pair[0]), jnp.where(odd, pair[0], pair[1])]
        return jnp.concatenate(
            [lax.ppermute(part, AXES, moves[step]) for step, part in enumerate(even_first)],
            axis=0,
        )

    def from_packs(rows):
        parts = [
            lax.ppermute(
                rows[step * row_count : (step + 1) * row_count], AXES, back(moves[step])
            )
            for step in range(2)
        ]
        return jnp.stack(
            [jnp.where(odd, parts[1], parts[0]), jnp.where(odd, parts[0], parts[1])]
        )

    def gather(shard):
        return lax.all_gather(shard, AXES, axis=0, tiled=True)

    blocks = row_count // BLOCK
    own_layout = lax.dynamic_slice_in_dim(block_layout[:, 0], place * blocks, blocks, axis=1)
    own_ids = jnp.take_along_axis(
        image_ids[:, 0].reshape(image_ids.shape[0], -1, BLOCK), own_layout[..., None], axis=1
    ).reshape(-1, row_count)

    x_low = to_packs(tokens)
    sizes = [vector.shape[0] for vector in vectors]
    fetched = gather(jnp.concatenate(vectors)[None])
    ends, start = [], 0
    for size in sizes:
        ends.append((start, start + size))
        start += size
    (
        gain_attn,
        shift_attn,
        bias_query,
        bias_value,
        bias_out,
        scale_attn,
        gain_mlp,
        shift_mlp,
        bias_up,
        bias_down,
        scale_mlp,
    ) = [fetched[:, low:high].reshape(-1).astype(jnp.float32) for low, high in ends]
    qkv_w = gather(qkv_weight)
    out_w = gather(out_weight)
    up_w = gather(up_weight)
    down_w = gather(down_weight)

    ids = to_packs(own_ids)
    id_sets = [ids] + [lax.ppermute(ids, AXES, perm) for perm in rounds]
    spare = jnp.arange(PAIR, dtype=jnp.int32)[None, :] % HEAD_DIM
    query_mask = (spare == ids[:, None]).astype(jnp.bfloat16)
    key_masks = [
        jnp.where((spare < ID_LANES) & (spare != each[:, None]), MASKED, 0.0).astype(jnp.bfloat16)
        for each in id_sets
    ]

    x_rows = x_low.astype(jnp.float32)
    normed_one, unit_one, inv_one = norm_parts(x_rows, gain_attn, shift_attn)
    normed_one_low = normed_one.astype(jnp.bfloat16)
    qkv_bias = jnp.concatenate([bias_query, jnp.zeros_like(bias_query), bias_value])
    qkv_rows = (
        jnp.dot(normed_one_low, qkv_w, preferred_element_type=jnp.float32) + qkv_bias
    ).astype(jnp.bfloat16)
    own_kv = qkv_rows[:, width:]
    others = [lax.ppermute(own_kv, AXES, perm) for perm in rounds]
    mixed_low, lse = attend(qkv_rows, others, query_mask, key_masks)
    branch_one = jnp.dot(mixed_low, out_w, preferred_element_type=jnp.float32) + bias_out
    resid = x_rows + scale_attn * branch_one
    normed_two, unit_two, inv_two = norm_parts(resid, gain_mlp, shift_mlp)
    normed_two_low = normed_two.astype(jnp.bfloat16)
    hidden = jnp.dot(normed_two_low, up_w, preferred_element_type=jnp.float32) + bias_up
    active, slope = gelu_parts(hidden)
    active_low = active.astype(jnp.bfloat16)
    branch_two = jnp.dot(active_low, down_w, preferred_element_type=jnp.float32) + bias_down
    block_out = from_packs((resid + scale_mlp * branch_two).astype(jnp.bfloat16))

    def reduce(total):
        return lax.psum_scatter(
            total.astype(jnp.bfloat16), AXES, scatter_dimension=0, tiled=True
        ).astype(jnp.float32)

    grad_y = to_packs(cotangent).astype(jnp.float32)
    d_scale_mlp = jnp.sum(grad_y * branch_two, axis=0)
    grad_two = (scale_mlp * grad_y).astype(jnp.bfloat16)
    d_bias_down = jnp.sum(grad_two.astype(jnp.float32), axis=0)
    d_down = reduce(outer_sum(active_low, grad_two))
    grad_hidden = (back_dot(grad_two, down_w) * slope).astype(jnp.bfloat16)
    d_bias_up = jnp.sum(grad_hidden.astype(jnp.float32), axis=0)
    d_up = reduce(outer_sum(normed_two_low, grad_hidden))
    grad_norm_two = back_dot(grad_hidden, up_w)
    d_gain_mlp = jnp.sum(grad_norm_two * unit_two, axis=0)
    d_shift_mlp = jnp.sum(grad_norm_two, axis=0)
    grad_resid = grad_y + norm_back(grad_norm_two, unit_two, inv_two, gain_mlp)
    d_scale_attn = jnp.sum(grad_resid * branch_one, axis=0)
    grad_one = (scale_attn * grad_resid).astype(jnp.bfloat16)
    d_bias_out = jnp.sum(grad_one.astype(jnp.float32), axis=0)
    d_out = reduce(outer_sum(mixed_low, grad_one))
    grad_mixed = back_dot(grad_one, out_w).astype(jnp.bfloat16)

    prior, returned = None, []
    for perm, key_value, key_mask in zip(rounds, others, key_masks[1:]):
        prior, part_k, part_v = attend_back(
            qkv_rows, grad_mixed, mixed_low, lse, query_mask, key_value, key_mask, prior, False, False
        )
        returned.append(
            (lax.ppermute(part_k, AXES, back(perm)), lax.ppermute(part_v, AXES, back(perm)))
        )
    grad_q, grad_k, grad_v = attend_back(
        qkv_rows, grad_mixed, mixed_low, lse, query_mask, qkv_rows, key_masks[0], prior, True, True
    )
    grad_k = sum([part[0].astype(jnp.float32) for part in returned], grad_k.astype(jnp.float32))
    grad_v = sum([part[1].astype(jnp.float32) for part in returned], grad_v.astype(jnp.float32))
    grad_qkv = jnp.concatenate(
        [grad_q, grad_k.astype(jnp.bfloat16), grad_v.astype(jnp.bfloat16)], axis=1
    )
    d_qkv_bias = jnp.sum(grad_qkv.astype(jnp.float32), axis=0)
    d_qkv = reduce(outer_sum(normed_one_low, grad_qkv))
    grad_norm_one = back_dot(grad_qkv, qkv_w)
    d_gain_attn = jnp.sum(grad_norm_one * unit_one, axis=0)
    d_shift_attn = jnp.sum(grad_norm_one, axis=0)
    grad_x = grad_resid + norm_back(grad_norm_one, unit_one, inv_one, gain_attn)
    token_grad = from_packs(grad_x.astype(jnp.bfloat16))
    vector_grads = (
        d_gain_attn,
        d_shift_attn,
        d_qkv_bias[:width],
        d_qkv_bias[2 * width :],
        d_bias_out,
        d_scale_attn,
        d_gain_mlp,
        d_shift_mlp,
        d_bias_up,
        d_bias_down,
        d_scale_mlp,
    )
    stacked = jnp.concatenate([grad.reshape(devices, -1) for grad in vector_grads], axis=1)
    summed = lax.psum_scatter(stacked, AXES, scatter_dimension=0, tiled=True)[0]
    return (block_out, token_grad, d_qkv, d_out, d_up, d_down) + tuple(
        summed[low:high] for low, high in ends
    )


def solution(mesh):
    rows = P(None, AXES, None)
    column = P(None, "gy", None)
    matrix = P(AXES, None)
    vector = P(AXES)
    return jax.shard_map(
        functools.partial(shards, mesh.shape["gx"], mesh.shape["gy"]),
        mesh=mesh,
        in_specs=(rows, rows, column, column) + (matrix,) * 4 + (vector,) * 11,
        out_specs=(rows, rows) + (matrix,) * 4 + (vector,) * 11,
        check_vma=False,
    )
```

time: 1580 us -> 945 us (0.60)
  waiting for transfers between devices: 886 us -> 473 us
  matrix products: 392 us -> 124 us
  Pallas kernels: 0 us -> 97.9 us
  local copies, waits for them, and re-layouts: 97.4 us -> 17.8 us
  starting transfers between devices: 0.82 us -> 53 us
  other arithmetic: 59.1 us -> 23.2 us
    dot_general x28 -> x8, matrix products: 321 us -> 80.9 us  [dot32(): lax.dot_general(left, right, dims, preferred_element_type=jnp.float32)]
    reduce_scatter x4, waiting for transfers between devices: 545 us -> 341 us  [reduce(): lax.psum_scatter(total.astype(jnp.bfloat16), AXES, scatter_dimension=0, t...]
    all_gather x8 -> x4, waiting for transfers between devices: 239 us -> 119 us  [gather(): return lax.all_gather(shard, AXES, axis=0, tiled=True)]
    unnamed x20 -> x8, waiting for transfers between devices: 102 us -> 2.65 us
    pallas_call x0 -> x3, Pallas kernels: none -> 97.9 us  [the longest x2 58.4 us: attend_back(): pl.pallas_call(functools.partial(back_kernel, has_prior), grid=(pairs,),...]
    ppermute x0 -> x14, starting transfers between devices: none -> 52.7 us  [the longest x1 21.7 us: shards(): id_sets = [ids] + [lax.ppermute(ids, AXES, perm) for perm in rounds]]
    unnamed x2, blocking collectives: 84.6 us -> 134 us
    all_gather x1 -> x0, blocking collectives: 39.6 us -> none  [fetch_params(): lax.all_gather(up_bias, ('gx', 'gy'), axis=0, tiled=True)]
  transfers between devices with their start and end apart: 16 -> 22, of which waited for: 13 -> 8; matrix products, arithmetic and copies ran while one was open for 28% -> 12% of each run, Pallas kernels for 0% -> 10%
where the time goes in v1:
time: 945 us; the launch traced here: 938 us
  waiting for transfers between devices  473 us (50%)
  blocking collectives  134 us (14%)
  matrix products  124 us (13%)
  Pallas kernels  97.9 us (10%)
  starting transfers between devices  53 us (6%)
  other arithmetic  23.2 us (2%)
  local copies, waits for them, and re-layouts  17.8 us (2%)
  between operations  15.4 us (2%)
    reduce_scatter x4, waiting for transfers between devices, reduce(): lax.psum_scatter(total.astype(jnp.bfloat16), AXES, scatter_dimension=0, t...  341 us
    unnamed x2, blocking collectives  134 us
    all_gather x4, waiting for transfers between devices, gather(): return lax.all_gather(shard, AXES, axis=0, tiled=True)  119 us
    dot_general x8, matrix products, dot32(): lax.dot_general(left, right, dims, preferred_element_type=jnp.float32)  80.9 us
    pallas_call x2, Pallas kernels, attend_back(): pl.pallas_call(functools.partial(back_kernel, has_prior), grid=(pairs,),...  58.4 us
    pallas_call x1, Pallas kernels, attend(): pl.pallas_call(functools.partial(attend_kernel, group), grid=(pairs, 2),...  39.5 us
    ppermute x1, starting transfers between devices, shards(): id_sets = [ids] + [lax.ppermute(ids, AXES, perm) for perm in rounds]  21.7 us
  transfers between devices with their start and end apart: 22, of which 8 were waited for; matrix products, arithmetic and copies ran while one was open for 12% of the time, Pallas kernels for 10%

profile of v1, /device:TPU:0, one launch (start us, length us, event | category | flops | bytes accessed | tf_op | source)
XLA Modules:
  0.0 937.5 jit_solution(4370727199437675353)
XLA Ops:
  16.9 69.4 %all-reduce = bf16[14336]{0:T(1024)(128)(2,1)S(1)} all-reduce(bf16[14336]{0:T(1024)(128)(2,1)S(1)} %dynamic-update-slice), channel_id=2, replica_groups=mesh['gx'=4,'gy'=8] {'gx','gy'}, use_global_device_ids=true, to_apply=%add | all-reduce | flops 14336 | bytes 57344
  87.7 8.8 all-gather.6.cloned.1.call-done
  96.4 9.1 add_convert_fusion.refs_0_.refs_2_.refs_4_.refs_5_.refs_6_
  121.2 8.6 collective-permute-done.3
  129.9 21.7 %collective-permute-start.5 = (s32[768]{0:T(1024)S(1)}, s32[768]{0:T(1024)S(1)}, u32[]{:S(2)}, u32[]{:S(2)}) collective-permute-start(s32[768]{0:T(1024)S(1)} %constant_dynamic-update-slice_fusion.1), channel_id=1, source_target_pairs={{0,1},{1,0},{8,9},{9,8},{16,17},{17,16},{24,25},{25,24},{2,3},{3,2... | collective-permute-start | bytes 9224 | tf_op jit(solution)/shard_map/ppermute | solution.py:330
  152.7 39.5 %attend.1 = (bf16[768,1024]{1,0:T(8,128)(2,1)S(1)}, f32[768,1024]{1,0:T(8,128)}) custom-call(bf16[768,3072]{1,0:T(8,128)(2,1)} %copy-done.14, bf16[768,128]{1,0:T(8,128)(2,1)S(1)} %compare_convert_fusion.refs_1_.refs_4_, bf16[768,3072]{1,0:T(8,128)(2,1)} %copy-done.14, bf16[768,2048]{1,0:T(8,128)(2,1)} %collective-permute-done.4.refs_3_.refs_5_.refs_6_, ...), custom_call_target="tpu_custom_call" | custom-call | flops 9663676416 | bytes 12582912 | tf_op jit(solution)/shard_map/attend/pallas_call | solution.py:106
  200.3 47.2 %all-gather.10.cloned.1.call-done = bf16[1024,4096]{1,0:T(8,128)(2,1)} async-done(((bf16[32,4096]{1,0:T(8,128)(2,1)}), bf16[1024,4096]{1,0:T(8,128)(2,1)}) %all-gather.10.cloned.1.call-update) | async-done | bytes 8388624 | tf_op jit(solution)/shard_map/all_gather | solution.py:296
  247.4 15.3 %multiply_convert_fusion = (bf16[768,4096]{1,0:T(8,128)(2,1)}, f32[768,4096]{1,0:T(8,128)}) fusion(f32[4096]{0:T(1024)S(1)} %fusion.25, bf16[1024,4096]{1,0:T(8,128)(2,1)} %all-gather.10.cloned.1.call-done, f32[768,1024]{1,0:T(8,128)} %copy-done.12, f32[1024]{0:T(1024)S(1)} %reshape.317, f32[1024]{0:T(1024)S(1)} %reshape.316, f32[768]{0:T(1024)S(1)} %add_rsqrt_fusion, ...), kind=kOutput, calls=%fused_computation.9 | convolution fusion | flops 6465257472 | bytes 30439424 | tf_op jit(solution)/shard_map/dot_general | solution.py:352
  262.7 63.4 %all-gather.12.cloned.1.call-done = bf16[4096,1024]{1,0:T(8,128)(2,1)} async-done(((bf16[128,1024]{1,0:T(8,128)(2,1)}), bf16[4096,1024]{1,0:T(8,128)(2,1)}) %all-gather.12.cloned.1.call-update) | async-done | bytes 8388624 | tf_op jit(solution)/shard_map/all_gather | solution.py:296
  326.2 16.4 %convert_reduce_fusion = (f32[4096]{0:T(1024)}, bf16[768,4096]{1,0:T(8,128)(2,1)}) fusion(f32[768,4096]{1,0:T(8,128)} %get-tuple-element.92, f32[4096]{0:T(1024)S(1)} %fusion.25, bf16[4096,1024]{1,0:T(8,128)(2,1)} %all-gather.12.cloned.1.call-done, f32[1024]{0:T(1024)S(1)} %reshape.315, bf16[384,1024]{1,0:T(8,128)(2,1)} %collective-permute-done.9, ...), kind=kOutput, calls=%fused_computation.8 | convolution fusion | flops 6488059904 | bytes 28872704 | tf_op jit(solution)/shard_map/dot_general | solution.py:26
  342.6 13.7 %multiply_reduce_fusion = (f32[1024]{0:T(1024)}, f32[768]{0:T(1024)S(1)}, f32[768]{0:T(1024)S(1)}, f32[1024]{0:T(1024)}, f32[768,1024]{1,0:T(8,128)}) fusion(f32[768,1024]{1,0:T(8,128)S(1)} %copy-done.13, f32[768]{0:T(1024)S(1)} %add_rsqrt_fusion, f32[768]{0:T(1024)S(1)} %broadcast_multiply_fusion.4, f32[1024]{0:T(1024)S(1)} %reshape.316, ...), kind=kOutput, calls=%fused_computation.41 | convolution fusion | flops 6449524736 | bytes 20996096 | tf_op jit(solution)/shard_map/dot_general | solution.py:26
  356.4 12.6 %fusion.22 = (f32[1024]{0:T(1024)}, f32[1024]{0:T(1024)}, bf16[768,1024]{1,0:T(8,128)(2,1)}, f32[1024]{0:T(1024)}, f32[768,1024]{1,0:T(8,128)S(1)}) fusion(f32[1024]{0:T(1024)S(1)} %reshape.319, bf16[384,1024]{1,0:T(8,128)(2,1)} %collective-permute-done.9, bf16[384,1024]{1,0:T(8,128)(2,1)} %collective-permute-done.8, f32[1024]{0:T(1024)S(1)} %reshape.315, ...), kind=kOutput, calls=%fused_computation.39 | convolution fusion | flops 6462108672 | bytes 30449664 | tf_op jit(solution)/shard_map/dot_general | solution.py:355
  380.7 29.2 %attend_back.2 = (f32[768,1024]{1,0:T(8,128)}, bf16[768,1024]{1,0:T(8,128)(2,1)S(1)}, bf16[768,1024]{1,0:T(8,128)(2,1)S(1)}) custom-call(bf16[768,3072]{1,0:T(8,128)(2,1)} %copy-done.14, bf16[768,1024]{1,0:T(8,128)(2,1)} %convolution_convert_fusion.4.refs_1_, bf16[768,1024]{1,0:T(8,128)(2,1)} %copy-done.2, f32[768,1024]{1,0:T(8,128)} %get-tuple-element.26.refs_3_, ...), custom_call_target="tpu_custom_call" | custom-call | flops 12079595520 | bytes 15728640 | tf_op jit(solution)/shard_map/attend_back/pallas_call | solution.py:206
  410.4 29.2 %attend_back.3 = (bf16[768,1024]{1,0:T(8,128)(2,1)S(1)}, bf16[768,1024]{1,0:T(8,128)(2,1)S(1)}, bf16[768,1024]{1,0:T(8,128)(2,1)}) custom-call(bf16[768,3072]{1,0:T(8,128)(2,1)} %copy-done.14, bf16[768,1024]{1,0:T(8,128)(2,1)} %convolution_convert_fusion.4.refs_1_, bf16[768,1024]{1,0:T(8,128)(2,1)} %copy-done.2, f32[768,1024]{1,0:T(8,128)} %get-tuple-element.26.refs_3_, ...), custom_call_target="tpu_custom_call" | custom-call | flops 12079595520 | bytes 15728640 | tf_op jit(solution)/shard_map/attend_back/pallas_call | solution.py:206
  444.2 8.4 convolution_convert_fusion.2
  453.3 12.7 %convolution_convert_fusion.1 = bf16[1024,4096]{1,0:T(8,128)(2,1)} fusion(bf16[768,4096]{1,0:T(8,128)(2,1)} %get-tuple-element.96, f32[768,1024]{1,0:T(8,128)} %copy-done.12, f32[1024]{0:T(1024)S(1)} %copy-done.31, f32[1024]{0:T(1024)S(1)} %copy-done.29, f32[768]{0:T(1024)S(1)} %copy-done.38, f32[768]{0:T(1024)S(1)} %copy-done.22), kind=kOutput, calls=%fused_computation.14 | convolution fusion | flops 6450577408 | bytes 17840128 | tf_op jit(solution)/shard_map/dot_general | solution.py:26
  466.7 11.2 %convolution_convert_fusion = bf16[4096,1024]{1,0:T(8,128)(2,1)} fusion(bf16[768,4096]{1,0:T(8,128)(2,1)} %get-tuple-element.91, f32[1024]{0:T(1024)S(1)} %copy-done.27, bf16[384,1024]{1,0:T(8,128)(2,1)} %collective-permute-done.9, bf16[384,1024]{1,0:T(8,128)(2,1)} %collective-permute-done.8), kind=kOutput, calls=%fused_computation.13 | convolution fusion | flops 6451363840 | bytes 16257024 | tf_op jit(solution)/shard_map/dot_general | solution.py:26
  480.7 7.4 collective-permute-start.7
  488.6 10.2 %fusion.19 = (f32[1024]{0:T(1024)S(1)}, f32[768]{0:T(1024)S(1)}, f32[768]{0:T(1024)S(1)}, f32[1024]{0:T(1024)S(1)}, f32[768,1024]{1,0:T(8,128)S(1)}) fusion(f32[768]{0:T(1024)S(1)} %copy-done.20, f32[768]{0:T(1024)S(1)} %broadcast_multiply_fusion.5, bf16[384,1024]{1,0:T(8,128)(2,1)S(1)} %copy-done.6, bf16[384,1024]{1,0:T(8,128)(2,1)S(1)} %copy-done.8, ...), kind=kOutput, calls=%fused_computation.36 | convolution fusion | flops 4856213504 | bytes 15753216 | tf_op jit(solution)/shard_map/dot_general | solution.py:26
  501.9 7.6 collective-permute-start.13
  511.9 64.4 %all-reduce.1 = f32[32,448]{1,0:T(8,128)S(1)} all-reduce(f32[32,448]{1,0:T(8,128)S(1)} %concatenate.27), channel_id=7, replica_groups=mesh['gx'=4,'gy'=8] {'gx','gy'}, use_global_device_ids=true, to_apply=%region_22.23.clone | all-reduce | flops 14336 | bytes 114688
  583.7 47.2 %reduce-scatter.5.cloned.1.call-done = bf16[32,3072]{1,0:T(8,128)(2,1)} async-done(((bf16[1024,3072]{1,0:T(8,128)(2,1)}), bf16[32,3072]{1,0:T(8,128)(2,1)}) %reduce-scatter.5.cloned.1.call-update) | async-done | bytes 196624 | tf_op jit(solution)/shard_map/reduce_scatter | solution.py:359
  632.6 148.9 %reduce-scatter.9.cloned.1.call-done = bf16[32,4096]{1,0:T(8,128)(2,1)} async-done(((bf16[1024,4096]{1,0:T(8,128)(2,1)}), bf16[32,4096]{1,0:T(8,128)(2,1)}) %reduce-scatter.9.cloned.1.call-update) | async-done | bytes 262160 | tf_op jit(solution)/shard_map/reduce_scatter | solution.py:359
  783.3 145.1 %reduce-scatter.11.cloned.1.call-done = bf16[128,1024]{1,0:T(8,128)(2,1)} async-done(((bf16[4096,1024]{1,0:T(8,128)(2,1)}), bf16[128,1024]{1,0:T(8,128)(2,1)}) %reduce-scatter.11.cloned.1.call-update) | async-done | bytes 262160 | tf_op jit(solution)/shard_map/reduce_scatter | solution.py:359
  (227 shorter events, 74.9 us)
Async XLA Ops:
  7.3 89.1 %all-gather.6.cloned.1.call-start = ((), (), s32[]{:S(2)}) async-start(), calls=%async_computation.4 | async-start | bytes 6488064 | tf_op jit(solution)/shard_map/all_gather | solution.py:296
  8.1 184.2 %all-gather.8.cloned.1.call-start = ((), (), s32[]{:S(2)}) async-start(), calls=%async_computation.5 | async-start | bytes 2162688 | tf_op jit(solution)/shard_map/all_gather | solution.py:296
  8.8 238.6 %all-gather.10.cloned.1.call-start = ((), (), s32[]{:S(2)}) async-start(), calls=%async_computation.6 | async-start | bytes 8650752 | tf_op jit(solution)/shard_map/all_gather | solution.py:296
  9.5 316.6 %all-gather.12.cloned.1.call-start = ((), (), s32[]{:S(2)}) async-start(), calls=%async_computation.7 | async-start | bytes 8650752 | tf_op jit(solution)/shard_map/all_gather | solution.py:296
  10.1 572.1 %reduce-scatter.7.cloned.1.call-start = ((), (), s32[]{:S(2)}) async-start(), calls=%async_computation.9 | async-start | bytes 2162688 | tf_op jit(solution)/shard_map/reduce_scatter | solution.py:359
  11.7 75.1 %collective-permute-start.1 = (bf16[384,1024]{1,0:T(8,128)(2,1)S(1)}, bf16[384,1024]{1,0:T(8,128)(2,1)S(1)}, u32[]{:S(2)}, u32[]{:S(2)}) collective-permute-start(bf16[384,1024]{1,0:T(8,128)(2,1)S(1)} %get-tuple-element.63), channel_id=1, source_target_pairs={{0,16},{1,24},{2,18},{3,26},{4,20},{5,28},{6,22},{7,30},{8,0},{9,8... | collective-permute-start | bytes 2359304 | tf_op jit(solution)/shard_map/ppermute | solution.py:280
  15.8 71.1 %collective-permute-start = (bf16[384,1024]{1,0:T(8,128)(2,1)S(1)}, bf16[384,1024]{1,0:T(8,128)(2,1)S(1)}, u32[]{:S(2)}, u32[]{:S(2)}) collective-permute-start(bf16[384,1024]{1,0:T(8,128)(2,1)S(1)} %get-tuple-element.62), channel_id=1, source_target_pairs={{0,0},{1,8},{2,2},{3,10},{4,4},{5,12},{6,6},{7,14},{8,16},{9,24},{... | collective-permute-start | bytes 2359304 | tf_op jit(solution)/shard_map/ppermute | solution.py:280
  107.5 45.2 %collective-permute-start.4 = (bf16[768,2048]{1,0:T(8,128)(2,1)}, bf16[768,2048]{1,0:T(8,128)(2,1)}, u32[]{:S(2)}, u32[]{:S(2)}) collective-permute-start(bf16[768,2048]{1,0:T(8,128)(2,1)} %slice.217), channel_id=1, source_target_pairs={{0,1},{1,0},{8,9},{9,8},{16,17},{17,16},{24,25},{25,24},{2,3},{3,2... | collective-permute-start | bytes 9437192 | tf_op jit(solution)/shard_map/ppermute | solution.py:346
  109.4 153.4 %collective-permute-start.9 = (bf16[384,1024]{1,0:T(8,128)(2,1)}, bf16[384,1024]{1,0:T(8,128)(2,1)}, u32[]{:S(2)}, u32[]{:S(2)}) collective-permute-start(bf16[384,1024]{1,0:T(8,128)(2,1)} %get-tuple-element.57), channel_id=1, source_target_pairs={{0,16},{1,24},{2,18},{3,26},{4,20},{5,28},{6,22},{7,30},{8,0},{9,8... | collective-permute-start | bytes 2359304 | tf_op jit(solution)/shard_map/ppermute | solution.py:280
  111.2 151.6 %collective-permute-start.8 = (bf16[384,1024]{1,0:T(8,128)(2,1)}, bf16[384,1024]{1,0:T(8,128)(2,1)}, u32[]{:S(2)}, u32[]{:S(2)}) collective-permute-start(bf16[384,1024]{1,0:T(8,128)(2,1)} %get-tuple-element.56), channel_id=1, source_target_pairs={{0,0},{1,8},{2,2},{3,10},{4,4},{5,12},{6,6},{7,14},{8,16},{9,24},{... | collective-permute-start | bytes 2359304 | tf_op jit(solution)/shard_map/ppermute | solution.py:280
  119.5 1.7 collective-permute-start.2
  120.2 9.7 %collective-permute-start.3 = (s32[384]{0:T(512)S(1)}, s32[384]{0:T(512)S(1)}, u32[]{:S(2)}, u32[]{:S(2)}) collective-permute-start(s32[384]{0:T(512)S(1)} %get-tuple-element.86), channel_id=1, source_target_pairs={{0,16},{1,24},{2,18},{3,26},{4,20},{5,28},{6,22},{7,30},{8,0},{9,8... | collective-permute-start | bytes 4616 | tf_op jit(solution)/shard_map/ppermute | solution.py:280
  120.9 235.4 %copy-start.26 = (f32[1024]{0:T(1024)}, f32[1024]{0:T(1024)S(1)}, u32[]{:S(2)}) copy-start(f32[1024]{0:T(1024)S(1)} %reshape.315) | copy-start | bytes 12292
  129.9 22.5 %collective-permute-start.5 = (s32[768]{0:T(1024)S(1)}, s32[768]{0:T(1024)S(1)}, u32[]{:S(2)}, u32[]{:S(2)}) collective-permute-start(s32[768]{0:T(1024)S(1)} %constant_dynamic-update-slice_fusion.1), channel_id=1, source_target_pairs={{0,1},{1,0},{8,9},{9,8},{16,17},{17,16},{24,25},{25,24},{2,3},{3,2... | collective-permute-start | bytes 9224 | tf_op jit(solution)/shard_map/ppermute | solution.py:330
  375.6 255.4 %reduce-scatter.5.cloned.1.call-start = ((), (), s32[]{:S(2)}) async-start(), calls=%async_computation.8 | async-start | bytes 6488064 | tf_op jit(solution)/shard_map/reduce_scatter | solution.py:359
  409.9 29.7 %collective-permute-start.11 = (bf16[768,1024]{1,0:T(8,128)(2,1)S(1)}, bf16[768,1024]{1,0:T(8,128)(2,1)S(1)}, u32[]{:S(2)}, u32[]{:S(2)}) collective-permute-start(bf16[768,1024]{1,0:T(8,128)(2,1)S(1)} %get-tuple-element.32), channel_id=1, source_target_pairs={{1,0},{0,1},{9,8},{8,9},{17,16},{16,17},{25,24},{24,25},{3,2},{2,3... | collective-permute-start | bytes 4718600 | tf_op jit(solution)/shard_map/ppermute | solution.py:387
  410.1 31.6 %collective-permute-start.10 = (bf16[768,1024]{1,0:T(8,128)(2,1)S(1)}, bf16[768,1024]{1,0:T(8,128)(2,1)S(1)}, u32[]{:S(2)}, u32[]{:S(2)}) collective-permute-start(bf16[768,1024]{1,0:T(8,128)(2,1)S(1)} %get-tuple-element.30), channel_id=1, source_target_pairs={{1,0},{0,1},{9,8},{8,9},{17,16},{16,17},{25,24},{24,25},{3,2},{2,3... | collective-permute-start | bytes 4718600 | tf_op jit(solution)/shard_map/ppermute | solution.py:387
  452.6 328.9 %reduce-scatter.9.cloned.1.call-start = ((), (), s32[]{:S(2)}) async-start(), calls=%async_computation.10 | async-start | bytes 8650752 | tf_op jit(solution)/shard_map/reduce_scatter | solution.py:359
  466.0 462.4 %reduce-scatter.11.cloned.1.call-start = ((), (), s32[]{:S(2)}) async-start(), calls=%async_computation.11 | async-start | bytes 8650752 | tf_op jit(solution)/shard_map/reduce_scatter | solution.py:359
  480.7 96.8 %collective-permute-start.7 = (bf16[384,1024]{1,0:T(8,128)(2,1)}, bf16[384,1024]{1,0:T(8,128)(2,1)}, u32[]{:S(2)}, u32[]{:S(2)}) collective-permute-start(bf16[384,1024]{1,0:T(8,128)(2,1)} %get-tuple-element.61), channel_id=1, source_target_pairs={{0,0},{8,1},{2,2},{10,3},{4,4},{12,5},{6,6},{14,7},{16,8},{24,9},{... | collective-permute-start | bytes 2359304 | tf_op jit(solution)/shard_map/ppermute | solution.py:286
  488.1 89.4 %collective-permute-start.6 = (bf16[384,1024]{1,0:T(8,128)(2,1)}, bf16[384,1024]{1,0:T(8,128)(2,1)}, u32[]{:S(2)}, u32[]{:S(2)}) collective-permute-start(bf16[384,1024]{1,0:T(8,128)(2,1)} %get-tuple-element.60), channel_id=1, source_target_pairs={{16,0},{24,1},{18,2},{26,3},{20,4},{28,5},{22,6},{30,7},{0,8},{8,9... | collective-permute-start | bytes 2359304 | tf_op jit(solution)/shard_map/ppermute | solution.py:286
  501.8 75.7 %collective-permute-start.12 = (bf16[384,1024]{1,0:T(8,128)(2,1)}, bf16[384,1024]{1,0:T(8,128)(2,1)}, u32[]{:S(2)}, u32[]{:S(2)}) collective-permute-start(bf16[384,1024]{1,0:T(8,128)(2,1)} %get-tuple-element.54), channel_id=1, source_target_pairs={{16,0},{24,1},{18,2},{26,3},{20,4},{28,5},{22,6},{30,7},{0,8},{8,9... | collective-permute-start | bytes 2359304 | tf_op jit(solution)/shard_map/ppermute | solution.py:286
  501.9 75.7 %collective-permute-start.13 = (bf16[384,1024]{1,0:T(8,128)(2,1)}, bf16[384,1024]{1,0:T(8,128)(2,1)}, u32[]{:S(2)}, u32[]{:S(2)}) collective-permute-start(bf16[384,1024]{1,0:T(8,128)(2,1)} %get-tuple-element.55), channel_id=1, source_target_pairs={{0,0},{8,1},{2,2},{10,3},{4,4},{12,5},{6,6},{14,7},{16,8},{24,9},{... | collective-permute-start | bytes 2359304 | tf_op jit(solution)/shard_map/ppermute | solution.py:286
  579.6 350.6 %copy-start.1 = (s32[2,1,1536]{2,1,0:T(1,128)S(1)}, s32[2,1,1536]{2,1,0:T(1,128)}, u32[]{:S(2)}) copy-start(s32[2,1,1536]{2,1,0:T(1,128)} %param.21) | copy-start | bytes 36868
  (51 other events, 1412.2 us)
Sparse Core Ops, SparseCore 0:
  11.0 85.3 all-gather.5
  99.3 68.8 all-gather.7
  171.1 76.2 all-gather.9
  250.2 75.9 all-gather.11
  375.7 136.9 reduce-scatter.6
  519.2 111.7 reduce-scatter.4
  633.2 148.2 reduce-scatter.8
  783.9 144.5 reduce-scatter.10

commit v2 on v1

--- a/solution.py
+++ b/solution.py
@@ -321,10 +321,17 @@
         bias_down,
         scale_mlp,
     ) = [fetched[:, low:high].reshape(-1).astype(jnp.float32) for low, high in ends]
-    qkv_w = gather(qkv_weight)
-    out_w = gather(out_weight)
-    up_w = gather(up_weight)
-    down_w = gather(down_weight)
+    shard_rows = qkv_weight.shape[0]
+    merged = gather(
+        jnp.concatenate(
+            [qkv_weight, out_weight, up_weight, down_weight.reshape(shard_rows, -1)], axis=1
+        )
+    )
+    cuts = [3 * width, 4 * width, 8 * width]
+    qkv_w = merged[:, : cuts[0]]
+    out_w = merged[:, cuts[0] : cuts[1]]
+    up_w = merged[:, cuts[1] : cuts[2]]
+    down_w = merged[:, cuts[2] :].reshape(-1, width)
 
     ids = to_packs(own_ids)
     id_sets = [ids] + [lax.ppermute(ids, AXES, perm) for perm in rounds]
@@ -364,10 +371,10 @@
     d_scale_mlp = jnp.sum(grad_y * branch_two, axis=0)
     grad_two = (scale_mlp * grad_y).astype(jnp.bfloat16)
     d_bias_down = jnp.sum(grad_two.astype(jnp.float32), axis=0)
-    d_down = reduce(outer_sum(active_low, grad_two))
+    sum_down = outer_sum(active_low, grad_two).astype(jnp.bfloat16)
     grad_hidden = (back_dot(grad_two, down_w) * slope).astype(jnp.bfloat16)
     d_bias_up = jnp.sum(grad_hidden.astype(jnp.float32), axis=0)
-    d_up = reduce(outer_sum(normed_two_low, grad_hidden))
+    sum_up = outer_sum(normed_two_low, grad_hidden).astype(jnp.bfloat16)
     grad_norm_two = back_dot(grad_hidden, up_w)
     d_gain_mlp = jnp.sum(grad_norm_two * unit_two, axis=0)
     d_shift_mlp = jnp.sum(grad_norm_two, axis=0)
@@ -375,7 +382,11 @@
     d_scale_attn = jnp.sum(grad_resid * branch_one, axis=0)
     grad_one = (scale_attn * grad_resid).astype(jnp.bfloat16)
     d_bias_out = jnp.sum(grad_one.astype(jnp.float32), axis=0)
-    d_out = reduce(outer_sum(mixed_low, grad_one))
+    sum_out = outer_sum(mixed_low, grad_one).astype(jnp.bfloat16)
+    early = reduce(jnp.concatenate([sum_out, sum_up, sum_down.reshape(width, -1)], axis=1))
+    d_out = early[:, :width]
+    d_up = early[:, width : 5 * width]
+    d_down = early[:, 5 * width :].reshape(down_weight.shape)
     grad_mixed = back_dot(grad_one, out_w).astype(jnp.bfloat16)
 
     prior, returned = None, []

time: 945 us -> 815 us (0.86)
  waiting for transfers between devices: 473 us -> 273 us
  local copies, waits for them, and re-layouts: 17.8 us -> 58.7 us
  blocking collectives: 134 us -> 157 us
  other arithmetic: 23.2 us -> 34.3 us
    reduce_scatter x4 -> x2, waiting for transfers between devices: 341 us -> 169 us  [reduce(): lax.psum_scatter(total.astype(jnp.bfloat16), AXES, scatter_dimension=0, t...]
    reshape x0 -> x4, local copies, waits for them, and re-layouts: none -> 30.5 us  [the longest x1 14.3 us: shards(): sum_down.reshape(width, -1)]
    all_gather x4 -> x1, waiting for transfers between devices: 119 us -> 91.4 us  [gather(): return lax.all_gather(shard, AXES, axis=0, tiled=True)]
    unnamed x2, blocking collectives: 134 us -> 157 us
    concatenate x0 -> x2, other arithmetic: none -> 17.5 us  [the longest x1 15.5 us: shards(): jnp.concatenate([sum_out, sum_up, sum_down.reshape(width, -1)], axis=1)]
    slice x0 -> x3, local copies, waits for them, and re-layouts: none -> 11.1 us  [the longest x1 7.73 us: shards(): down_w = merged[:, cuts[2]:].reshape(-1, width)]
  transfers between devices with their start and end apart: 22 -> 17, of which waited for: 8 -> 4; matrix products, arithmetic and copies ran while one was open for 12% -> 17% of each run, Pallas kernels for 10% -> 9%
where the time goes in v2:
time: 815 us; the launch traced here: 807 us
  waiting for transfers between devices  273 us (33%)
  blocking collectives  157 us (19%)
  matrix products  126 us (15%)
  Pallas kernels  97.9 us (12%)
  local copies, waits for them, and re-layouts  58.7 us (7%)
  starting transfers between devices  45 us (6%)
  other arithmetic  34.3 us (4%)
  between operations  15.1 us (2%)
    reduce_scatter x2, waiting for transfers between devices, reduce(): lax.psum_scatter(total.astype(jnp.bfloat16), AXES, scatter_dimension=0, t...  169 us
    unnamed x2, blocking collectives  157 us
    all_gather x1, waiting for transfers between devices, gather(): return lax.all_gather(shard, AXES, axis=0, tiled=True)  91.4 us
    dot_general x8, matrix products, dot32(): lax.dot_general(left, right, dims, preferred_element_type=jnp.float32)  82.8 us
    pallas_call x2, Pallas kernels, attend_back(): pl.pallas_call(functools.partial(back_kernel, has_prior), grid=(pairs,),...  58.4 us
    pallas_call x1, Pallas kernels, attend(): pl.pallas_call(functools.partial(attend_kernel, group), grid=(pairs, 2),...  39.5 us
  transfers between devices with their start and end apart: 17, of which 4 were waited for; matrix products, arithmetic and copies ran while one was open for 17% of the time, Pallas kernels for 9%

profile of v2, /device:TPU:0, one launch (start us, length us, event | category | flops | bytes accessed | tf_op | source)
XLA Modules:
  0.0 807.0 jit_solution(1872441614131839480)
XLA Ops:
  16.0 77.9 %all-reduce = bf16[14336]{0:T(1024)(128)(2,1)S(1)} all-reduce(bf16[14336]{0:T(1024)(128)(2,1)S(1)} %dynamic-update-slice), channel_id=2, replica_groups=mesh['gx'=4,'gy'=8] {'gx','gy'}, use_global_device_ids=true, to_apply=%add | all-reduce | flops 14336 | bytes 57344
  95.4 91.4 %all-gather.3.cloned.1.call-done = bf16[1024,12288]{1,0:T(8,128)(2,1)} async-done(((bf16[32,12288]{1,0:T(8,128)(2,1)}), bf16[1024,12288]{1,0:T(8,128)(2,1)}) %all-gather.3.cloned.1.call-update) | async-done | bytes 25165840 | tf_op jit(solution)/shard_map/all_gather | solution.py:296
  186.7 9.1 %add_convert_fusion.refs_0_.refs_2_.refs_4_.refs_5_.refs_6_ = bf16[768,3072]{1,0:T(8,128)(2,1)S(1)} fusion(f32[3072]{0:T(1024)S(1)} %pad_maximum_fusion.7, bf16[1024,12288]{1,0:T(8,128)(2,1)} %all-gather.3.cloned.1.call-done, f32[1024]{0:T(1024)S(1)} %reshape.327, f32[1024]{0:T(1024)S(1)} %reshape.326, f32[768]{0:T(1024)S(1)} %add_rsqrt_fusion.1, ...), kind=kOutput, calls=%fused_computation.13 | convolution fusion | flops 4843634688 | bytes 12609536 | tf_op jit(solution)/shard_map/dot_general | solution.py:350
  210.1 11.4 %collective-permute-done.3 = s32[384]{0:T(512)S(1)} collective-permute-done((s32[384]{0:T(512)S(1)}, s32[384]{0:T(512)S(1)}, u32[]{:S(2)}, u32[]{:S(2)}) %collective-permute-start.3) | collective-permute-done | bytes 1568 | tf_op jit(solution)/shard_map/ppermute | solution.py:280
  221.5 15.5 %collective-permute-start.5 = (s32[768]{0:T(1024)S(1)}, s32[768]{0:T(1024)S(1)}, u32[]{:S(2)}, u32[]{:S(2)}) collective-permute-start(s32[768]{0:T(1024)S(1)} %constant_dynamic-update-slice_fusion.1), channel_id=1, source_target_pairs={{0,1},{1,0},{8,9},{9,8},{16,17},{17,16},{24,25},{25,24},{2,3},{3,2... | collective-permute-start | bytes 9224 | tf_op jit(solution)/shard_map/ppermute | solution.py:337
  238.1 7.7 slice.254
  245.8 14.1 %reshape.311 = bf16[4096,1024]{1,0:T(8,128)(2,1)} reshape(bf16[1024,4096]{1,0:T(8,128)(2,1)} %slice.254) | data formatting | bytes 16777216 | tf_op jit(solution)/shard_map/reshape | solution.py:334
  259.9 39.5 %attend.1 = (bf16[768,1024]{1,0:T(8,128)(2,1)S(1)}, f32[768,1024]{1,0:T(8,128)}) custom-call(bf16[768,3072]{1,0:T(8,128)(2,1)} %copy-done.15, bf16[768,128]{1,0:T(8,128)(2,1)S(1)} %compare_convert_fusion.refs_1_.refs_4_, bf16[768,3072]{1,0:T(8,128)(2,1)} %copy-done.15, bf16[768,2048]{1,0:T(8,128)(2,1)} %collective-permute-done.4.refs_3_.refs_5_.refs_6_, ...), custom_call_target="tpu_custom_call" | custom-call | flops 9663676416 | bytes 12582912 | tf_op jit(solution)/shard_map/attend/pallas_call | solution.py:106
  305.8 15.3 %multiply_convert_fusion = (bf16[768,4096]{1,0:T(8,128)(2,1)}, f32[768,4096]{1,0:T(8,128)}) fusion(f32[4096]{0:T(1024)S(1)} %fusion.42, bf16[1024,12288]{1,0:T(8,128)(2,1)} %all-gather.3.cloned.1.call-done, f32[768,1024]{1,0:T(8,128)S(1)} %get-tuple-element.48, f32[1024]{0:T(1024)S(1)} %reshape.333, f32[1024]{0:T(1024)S(1)} %reshape.332, ...), kind=kOutput, calls=%fused_computation.10 | convolution fusion | flops 6465257472 | bytes 30439424 | tf_op jit(solution)/shard_map/dot_general | solution.py:359
  321.0 18.3 %convert_reduce_fusion = (f32[4096]{0:T(1024)}, bf16[768,4096]{1,0:T(8,128)(2,1)}) fusion(f32[768,4096]{1,0:T(8,128)} %get-tuple-element.94, f32[4096]{0:T(1024)S(1)} %fusion.42, bf16[4096,1024]{1,0:T(8,128)(2,1)S(1)} %bitcast.64, f32[1024]{0:T(1024)S(1)} %reshape.331, bf16[384,1024]{1,0:T(8,128)(2,1)} %collective-permute-done.9, ...), kind=kOutput, calls=%fused_computation.9 | convolution fusion | flops 6488059904 | bytes 28872704 | tf_op jit(solution)/shard_map/dot_general | solution.py:26
  339.4 13.8 %multiply_reduce_fusion = (f32[1024]{0:T(1024)}, f32[768]{0:T(1024)S(1)}, f32[768]{0:T(1024)S(1)}, f32[1024]{0:T(1024)}, f32[768,1024]{1,0:T(8,128)}) fusion(f32[768,1024]{1,0:T(8,128)S(1)} %get-tuple-element.48, f32[768]{0:T(1024)S(1)} %add_rsqrt_fusion, f32[768]{0:T(1024)S(1)} %broadcast_multiply_fusion.4, f32[1024]{0:T(1024)S(1)} %reshape.332, ...), kind=kOutput, calls=%fused_computation.50 | convolution fusion | flops 6449524736 | bytes 20996096 | tf_op jit(solution)/shard_map/dot_general | solution.py:26
  353.2 13.1 %fusion.32 = (f32[1024]{0:T(1024)}, f32[1024]{0:T(1024)}, bf16[768,1024]{1,0:T(8,128)(2,1)}, f32[1024]{0:T(1024)}, f32[768,1024]{1,0:T(8,128)S(1)}) fusion(f32[1024]{0:T(1024)S(1)} %reshape.335, bf16[384,1024]{1,0:T(8,128)(2,1)} %collective-permute-done.9, bf16[384,1024]{1,0:T(8,128)(2,1)} %collective-permute-done.8, f32[1024]{0:T(1024)S(1)} %reshape.331, ...), kind=kOutput, calls=%fused_computation.48 | convolution fusion | flops 6462108672 | bytes 30449664 | tf_op jit(solution)/shard_map/dot_general | solution.py:362
  372.6 29.1 %attend_back.2 = (f32[768,1024]{1,0:T(8,128)}, bf16[768,1024]{1,0:T(8,128)(2,1)S(1)}, bf16[768,1024]{1,0:T(8,128)(2,1)S(1)}) custom-call(bf16[768,3072]{1,0:T(8,128)(2,1)} %copy-done.15, bf16[768,1024]{1,0:T(8,128)(2,1)} %fusion.37.refs_1_, bf16[768,1024]{1,0:T(8,128)(2,1)} %copy-done.2, f32[768,1024]{1,0:T(8,128)} %get-tuple-element.26.refs_3_, ...), custom_call_target="tpu_custom_call" | custom-call | flops 12079595520 | bytes 15728640 | tf_op jit(solution)/shard_map/attend_back/pallas_call | solution.py:206
  402.2 29.2 %attend_back.3 = (bf16[768,1024]{1,0:T(8,128)(2,1)S(1)}, bf16[768,1024]{1,0:T(8,128)(2,1)S(1)}, bf16[768,1024]{1,0:T(8,128)(2,1)}) custom-call(bf16[768,3072]{1,0:T(8,128)(2,1)} %copy-done.15, bf16[768,1024]{1,0:T(8,128)(2,1)} %fusion.37.refs_1_, bf16[768,1024]{1,0:T(8,128)(2,1)} %copy-done.2, f32[768,1024]{1,0:T(8,128)} %get-tuple-element.26.refs_3_, ...), custom_call_target="tpu_custom_call" | custom-call | flops 12079595520 | bytes 15728640 | tf_op jit(solution)/shard_map/attend_back/pallas_call | solution.py:206
  435.4 8.3 %convolution_convert_fusion.2 = bf16[1024,3072]{1,0:T(8,128)(2,1)} fusion(f32[1024]{0:T(1024)S(1)} %copy-done.27, f32[1024]{0:T(1024)S(1)} %copy-done.20, f32[768]{0:T(1024)S(1)} %copy-done.22, f32[768]{0:T(1024)S(1)} %broadcast_multiply_fusion.5, bf16[768,1024]{1,0:T(8,128)(2,1)S(1)} %add_convert_fusion.1, bf16[768,1024]{1,0:T(8,128)(2,1)S(1)} %add_convert_fusion.2, ...), kind=kOutput, calls=%fused_computation.20 | convolution fusion | flops 4856217600 | bytes 12597248 | tf_op jit(solution)/shard_map/dot_general | solution.py:26
  444.5 11.5 %convolution_convert_fusion = bf16[4096,1024]{1,0:T(8,128)(2,1)} fusion(bf16[768,4096]{1,0:T(8,128)(2,1)} %get-tuple-element.93, f32[1024]{0:T(1024)S(1)} %copy-done.33, bf16[384,1024]{1,0:T(8,128)(2,1)} %collective-permute-done.9, bf16[384,1024]{1,0:T(8,128)(2,1)} %collective-permute-done.8), kind=kOutput, calls=%fused_computation.14 | convolution fusion | flops 6451363840 | bytes 16257024 | tf_op jit(solution)/shard_map/dot_general | solution.py:26
  455.9 14.3 %reshape.312 = bf16[1024,4096]{1,0:T(8,128)(2,1)} reshape(bf16[4096,1024]{1,0:T(8,128)(2,1)} %convolution_convert_fusion) | data formatting | bytes 16777216 | tf_op jit(solution)/shard_map/reshape | solution.py:386
  479.0 10.7 %convolution_convert_fusion.1 = bf16[1024,4096]{1,0:T(8,128)(2,1)S(1)} fusion(bf16[768,4096]{1,0:T(8,128)(2,1)} %get-tuple-element.98, f32[768,1024]{1,0:T(8,128)} %copy-done.14, f32[1024]{0:T(1024)S(1)} %copy-done.31, f32[1024]{0:T(1024)S(1)} %copy-done.29, f32[768]{0:T(1024)S(1)} %copy-done.40, f32[768]{0:T(1024)S(1)} %copy-done.24), kind=kOutput, calls=%fused_computation.15 | convolution fusion | flops 6450577408 | bytes 17840128 | tf_op jit(solution)/shard_map/dot_general | solution.py:26
  489.8 15.5 %pad_maximum_fusion = bf16[1024,9216]{1,0:T(8,128)(2,1)} fusion(bf16[1024,4096]{1,0:T(8,128)(2,1)} %reshape.312, bf16[1024,4096]{1,0:T(8,128)(2,1)S(1)} %convolution_convert_fusion.1, bf16[1024,1024]{1,0:T(8,128)(2,1)S(1)} %copy-done.6), kind=kLoop, calls=%fused_computation.2 | loop fusion | flops 56623104 | bytes 37748736 | tf_op jit(solution)/shard_map/concatenate | solution.py:386
  508.2 7.4 collective-permute-start.7
  516.3 9.7 %fusion.29 = (f32[1024]{0:T(1024)S(1)}, f32[768]{0:T(1024)S(1)}, f32[768]{0:T(1024)S(1)}, f32[1024]{0:T(1024)S(1)}, f32[768,1024]{1,0:T(8,128)S(1)}) fusion(f32[768]{0:T(1024)S(1)} %copy-done.22, f32[768]{0:T(1024)S(1)} %broadcast_multiply_fusion.5, bf16[384,1024]{1,0:T(8,128)(2,1)S(1)} %copy-done.8, bf16[384,1024]{1,0:T(8,128)(2,1)S(1)} %copy-done.10, ...), kind=kOutput, calls=%fused_computation.45 | convolution fusion | flops 4856213504 | bytes 15753216 | tf_op jit(solution)/shard_map/dot_general | solution.py:26
  529.1 7.6 collective-permute-start.13
  539.1 79.5 %all-reduce.1 = f32[32,448]{1,0:T(8,128)S(1)} all-reduce(f32[32,448]{1,0:T(8,128)S(1)} %concatenate.35), channel_id=5, replica_groups=mesh['gx'=4,'gy'=8] {'gx','gy'}, use_global_device_ids=true, to_apply=%region_20.21.clone | all-reduce | flops 14336 | bytes 114688
  626.5 169.2 %reduce-scatter.5.cloned.1.call-done = bf16[32,9216]{1,0:T(8,128)(2,1)} async-done(((bf16[1024,9216]{1,0:T(8,128)(2,1)}), bf16[32,9216]{1,0:T(8,128)(2,1)}) %reduce-scatter.5.cloned.1.call-update) | async-done | bytes 589840 | tf_op jit(solution)/shard_map/reduce_scatter | solution.py:366
  (224 shorter events, 72.7 us)
Async XLA Ops:
  7.2 196.1 %copy-start = (s32[2,1,1536]{2,1,0:T(1,128)S(1)}, s32[2,1,1536]{2,1,0:T(1,128)}, u32[]{:S(2)}) copy-start(s32[2,1,1536]{2,1,0:T(1,128)} %param.21) | copy-start | bytes 36868
  7.3 179.4 %all-gather.3.cloned.1.call-start = ((), (), s32[]{:S(2)}) async-start(), calls=%async_computation.2 | async-start | bytes 25952256 | tf_op jit(solution)/shard_map/all_gather | solution.py:296
  10.6 614.2 %reduce-scatter.3.cloned.1.call-start = ((), (), s32[]{:S(2)}) async-start(), calls=%async_computation.3 | async-start | bytes 6488064 | tf_op jit(solution)/shard_map/reduce_scatter | solution.py:366
  10.8 83.7 %collective-permute-start.1 = (bf16[384,1024]{1,0:T(8,128)(2,1)S(1)}, bf16[384,1024]{1,0:T(8,128)(2,1)S(1)}, u32[]{:S(2)}, u32[]{:S(2)}) collective-permute-start(bf16[384,1024]{1,0:T(8,128)(2,1)S(1)} %get-tuple-element.63), channel_id=1, source_target_pairs={{0,16},{1,24},{2,18},{3,26},{4,20},{5,28},{6,22},{7,30},{8,0},{9,8... | collective-permute-start | bytes 2359304 | tf_op jit(solution)/shard_map/ppermute | solution.py:280
  14.9 79.6 %collective-permute-start = (bf16[384,1024]{1,0:T(8,128)(2,1)S(1)}, bf16[384,1024]{1,0:T(8,128)(2,1)S(1)}, u32[]{:S(2)}, u32[]{:S(2)}) collective-permute-start(bf16[384,1024]{1,0:T(8,128)(2,1)S(1)} %get-tuple-element.62), channel_id=1, source_target_pairs={{0,0},{1,8},{2,2},{3,10},{4,4},{5,12},{6,6},{7,14},{8,16},{9,24},{... | collective-permute-start | bytes 2359304 | tf_op jit(solution)/shard_map/ppermute | solution.py:280
  94.4 101.4 %copy-start.26 = (f32[1024]{0:T(1024)}, f32[1024]{0:T(1024)S(1)}, u32[]{:S(2)}) copy-start(f32[1024]{0:T(1024)S(1)} %reshape.327) | copy-start | bytes 12292
  94.5 339.8 %copy-start.7 = (bf16[384,1024]{1,0:T(8,128)(2,1)}, bf16[384,1024]{1,0:T(8,128)(2,1)S(1)}, u32[]{:S(2)}) copy-start(bf16[384,1024]{1,0:T(8,128)(2,1)S(1)} %collective-permute-done.1) | copy-start | bytes 2359300
  94.5 339.8 %copy-start.9 = (bf16[384,1024]{1,0:T(8,128)(2,1)}, bf16[384,1024]{1,0:T(8,128)(2,1)S(1)}, u32[]{:S(2)}) copy-start(bf16[384,1024]{1,0:T(8,128)(2,1)S(1)} %collective-permute-done) | copy-start | bytes 2359300
  198.9 61.0 %collective-permute-start.4 = (bf16[768,2048]{1,0:T(8,128)(2,1)}, bf16[768,2048]{1,0:T(8,128)(2,1)}, u32[]{:S(2)}, u32[]{:S(2)}) collective-permute-start(bf16[768,2048]{1,0:T(8,128)(2,1)} %slice.246), channel_id=1, source_target_pairs={{0,1},{1,0},{8,9},{9,8},{16,17},{17,16},{24,25},{25,24},{2,3},{3,2... | collective-permute-start | bytes 9437192 | tf_op jit(solution)/shard_map/ppermute | solution.py:353
  200.2 120.8 %collective-permute-start.9 = (bf16[384,1024]{1,0:T(8,128)(2,1)}, bf16[384,1024]{1,0:T(8,128)(2,1)}, u32[]{:S(2)}, u32[]{:S(2)}) collective-permute-start(bf16[384,1024]{1,0:T(8,128)(2,1)} %get-tuple-element.57), channel_id=1, source_target_pairs={{0,16},{1,24},{2,18},{3,26},{4,20},{5,28},{6,22},{7,30},{8,0},{9,8... | collective-permute-start | bytes 2359304 | tf_op jit(solution)/shard_map/ppermute | solution.py:280
  201.7 119.3 %collective-permute-start.8 = (bf16[384,1024]{1,0:T(8,128)(2,1)S(1)}, bf16[384,1024]{1,0:T(8,128)(2,1)}, u32[]{:S(2)}, u32[]{:S(2)}) collective-permute-start(bf16[384,1024]{1,0:T(8,128)(2,1)S(1)} %get-tuple-element.56), channel_id=1, source_target_pairs={{0,0},{1,8},{2,2},{3,10},{4,4},{5,12},{6,6},{7,14},{8,16},{9,24},{... | collective-permute-start | bytes 2359304 | tf_op jit(solution)/shard_map/ppermute | solution.py:280
  204.2 5.9 collective-permute-start.2
  204.9 16.6 %collective-permute-start.3 = (s32[384]{0:T(512)S(1)}, s32[384]{0:T(512)S(1)}, u32[]{:S(2)}, u32[]{:S(2)}) collective-permute-start(s32[384]{0:T(512)S(1)} %get-tuple-element.88), channel_id=1, source_target_pairs={{0,16},{1,24},{2,18},{3,26},{4,20},{5,28},{6,22},{7,30},{8,0},{9,8... | collective-permute-start | bytes 4616 | tf_op jit(solution)/shard_map/ppermute | solution.py:280
  209.8 143.4 %copy-start.32 = (f32[1024]{0:T(1024)}, f32[1024]{0:T(1024)S(1)}, u32[]{:S(2)}) copy-start(f32[1024]{0:T(1024)S(1)} %reshape.331) | copy-start | bytes 12292
  210.0 143.2 %copy-start.28 = (f32[1024]{0:T(1024)}, f32[1024]{0:T(1024)S(1)}, u32[]{:S(2)}) copy-start(f32[1024]{0:T(1024)S(1)} %reshape.332) | copy-start | bytes 12292
  221.5 16.3 %collective-permute-start.5 = (s32[768]{0:T(1024)S(1)}, s32[768]{0:T(1024)S(1)}, u32[]{:S(2)}, u32[]{:S(2)}) collective-permute-start(s32[768]{0:T(1024)S(1)} %constant_dynamic-update-slice_fusion.1), channel_id=1, source_target_pairs={{0,1},{1,0},{8,9},{9,8},{16,17},{17,16},{24,25},{25,24},{2,3},{3,2... | collective-permute-start | bytes 9224 | tf_op jit(solution)/shard_map/ppermute | solution.py:337
  401.7 29.7 %collective-permute-start.11 = (bf16[768,1024]{1,0:T(8,128)(2,1)S(1)}, bf16[768,1024]{1,0:T(8,128)(2,1)S(1)}, u32[]{:S(2)}, u32[]{:S(2)}) collective-permute-start(bf16[768,1024]{1,0:T(8,128)(2,1)S(1)} %get-tuple-element.32), channel_id=1, source_target_pairs={{1,0},{0,1},{9,8},{8,9},{17,16},{16,17},{25,24},{24,25},{3,2},{2,3... | collective-permute-start | bytes 4718600 | tf_op jit(solution)/shard_map/ppermute | solution.py:398
  402.0 31.5 %collective-permute-start.10 = (bf16[768,1024]{1,0:T(8,128)(2,1)S(1)}, bf16[768,1024]{1,0:T(8,128)(2,1)S(1)}, u32[]{:S(2)}, u32[]{:S(2)}) collective-permute-start(bf16[768,1024]{1,0:T(8,128)(2,1)S(1)} %get-tuple-element.30), channel_id=1, source_target_pairs={{1,0},{0,1},{9,8},{8,9},{17,16},{16,17},{25,24},{24,25},{3,2},{2,3... | collective-permute-start | bytes 4718600 | tf_op jit(solution)/shard_map/ppermute | solution.py:398
  443.8 351.8 %reduce-scatter.5.cloned.1.call-start = ((), (), s32[]{:S(2)}) async-start(), calls=%async_computation.4 | async-start | bytes 19464192 | tf_op jit(solution)/shard_map/reduce_scatter | solution.py:366
  508.2 111.6 %collective-permute-start.7 = (bf16[384,1024]{1,0:T(8,128)(2,1)}, bf16[384,1024]{1,0:T(8,128)(2,1)}, u32[]{:S(2)}, u32[]{:S(2)}) collective-permute-start(bf16[384,1024]{1,0:T(8,128)(2,1)} %get-tuple-element.61), channel_id=1, source_target_pairs={{0,0},{8,1},{2,2},{10,3},{4,4},{12,5},{6,6},{14,7},{16,8},{24,9},{... | collective-permute-start | bytes 2359304 | tf_op jit(solution)/shard_map/ppermute | solution.py:286
  515.6 104.2 %collective-permute-start.6 = (bf16[384,1024]{1,0:T(8,128)(2,1)}, bf16[384,1024]{1,0:T(8,128)(2,1)}, u32[]{:S(2)}, u32[]{:S(2)}) collective-permute-start(bf16[384,1024]{1,0:T(8,128)(2,1)} %get-tuple-element.60), channel_id=1, source_target_pairs={{16,0},{24,1},{18,2},{26,3},{20,4},{28,5},{22,6},{30,7},{0,8},{8,9... | collective-permute-start | bytes 2359304 | tf_op jit(solution)/shard_map/ppermute | solution.py:286
  529.1 90.7 %collective-permute-start.12 = (bf16[384,1024]{1,0:T(8,128)(2,1)}, bf16[384,1024]{1,0:T(8,128)(2,1)}, u32[]{:S(2)}, u32[]{:S(2)}) collective-permute-start(bf16[384,1024]{1,0:T(8,128)(2,1)} %get-tuple-element.54), channel_id=1, source_target_pairs={{16,0},{24,1},{18,2},{26,3},{20,4},{28,5},{22,6},{30,7},{0,8},{8,9... | collective-permute-start | bytes 2359304 | tf_op jit(solution)/shard_map/ppermute | solution.py:286
  529.1 90.7 %collective-permute-start.13 = (bf16[384,1024]{1,0:T(8,128)(2,1)}, bf16[384,1024]{1,0:T(8,128)(2,1)}, u32[]{:S(2)}, u32[]{:S(2)}) collective-permute-start(bf16[384,1024]{1,0:T(8,128)(2,1)} %get-tuple-element.55), channel_id=1, source_target_pairs={{0,0},{8,1},{2,2},{10,3},{4,4},{12,5},{6,6},{14,7},{16,8},{24,9},{... | collective-permute-start | bytes 2359304 | tf_op jit(solution)/shard_map/ppermute | solution.py:286
  623.5 176.5 %copy-start.1 = (s32[2,1,1536]{2,1,0:T(1,128)S(1)}, s32[2,1,1536]{2,1,0:T(1,128)}, u32[]{:S(2)}) copy-start(s32[2,1,1536]{2,1,0:T(1,128)} %param.21) | copy-start | bytes 36868
  (48 other events, 749.9 us)
Sparse Core Ops, SparseCore 0:
  11.6 175.0 all-gather.2
  443.9 140.1 reduce-scatter.2
  591.7 203.9 reduce-scatter.4
